TPU v7x, 32 devices: a whole 2x2x4 slice. The times are simulated.
32 devices in a mesh: section: 2 (over core), blk: 4 (over y, x), mp: 4 (over z).
Axes of the slice: x: 2, y: 2, z: 4, core: 2. Of those that a mesh axis runs over, the one named last changes fastest.
Arguments:
- patches: bfloat16 [256, 5120], P('section'), may hold values from -6 to 6
- merge_gain: float32 [1280], replicated, may hold values from 0.25 to 1.75
- merge_first: bfloat16 [5120, 5120], P(None, ('blk', 'mp')), may hold values from -0.078125 to 0.078125
- merge_second: bfloat16 [5120, 4096], P(('blk', 'mp')), may hold values from -0.078125 to 0.078125
- text_embeds: bfloat16 [4, 256, 4096], P(None, 'blk', 'mp'), may hold values from -7 to 14
- positions: int32 [256], replicated, may hold values from 0 to 1023, as said below
- segments: int32 [1024], replicated, may hold values from 0 to 2, never falling along the last dimension, each value on 1 to 512 neighbouring positions
- norm_gain: float32 [2, 4096], P('section'), may hold values from 0.25 to 1.75
- query_weight: bfloat16 [2, 4096, 4096], P('section', 'blk', 'mp'), may hold values from -1 to 1
- keyval_weight: bfloat16 [2, 4096, 4, 2, 128], P('section', 'blk', 'mp'), may hold values from -1 to 1
- out_weight: bfloat16 [2, 4096, 4096], P('section', 'mp', 'blk'), may hold values from -0.09375 to 0.09375
Outputs:
- hidden: bfloat16 [2, 4, 256, 4096], P('section', None, 'blk', 'mp')
Inputs may be any that keep to these rules, and one draw needn't show every extreme that they name: `positions`: distinct and increasing.
All inputs are finite; a program needn't handle non-finite values.
Results may differ from a plain program's by a relative error of at most 0.015.
Values may be sent and summed in bfloat16 or wider, within the bound.
A program may use at most 128 MiB of HBM per device.

v0:
```python
import jax
import jax.numpy as jnp
from jax import lax
from jax.sharding import PartitionSpec as P

epsilon = 1e-06
rope_base = 1000000.0


def shifted(value, axis, by):
    size = lax.axis_size(axis)
    pairs = [(i, i + by) for i in range(size) if 0 <= i + by < size]
    return lax.ppermute(value, axis, pairs)


def rope_tables(where_at, head_size):
    steps_half = jnp.arange(head_size // 2).astype(jnp.float32)
    inverse = jnp.exp(-jnp.log(rope_base) * 2.0 * steps_half / head_size)
    angles = where_at.astype(jnp.float32)[:, None] * inverse[None, :]
    return (jnp.cos(angles), jnp.sin(angles))


def rotate(values, cosine, sine):
    half = values.shape[-1] // 2
    first = values[..., :half]
    second = values[..., half:]
    cosine = cosine[:, None, :]
    sine = sine[:, None, :]
    return jnp.concatenate(
        [first * cosine - second * sine, second * cosine + first * sine], axis=-1
    )


def local(
    patches,
    merge_gain,
    merge_first,
    merge_second,
    text_embeds,
    positions,
    segments,
    norm_gain,
    query_weight,
    keyval_weight,
    out_weight,
):
    count = patches.shape[0]
    width = merge_gain.shape[0]
    blocks = text_embeds.shape[0]
    rows_here = text_embeds.shape[1]
    slice_width = text_embeds.shape[2]
    seq_len = segments.shape[0]
    block_len = seq_len // blocks
    section_index = lax.axis_index("section")
    cycle_index = lax.axis_index("blk")
    model_index = lax.axis_index("mp")
    pieces = patches.astype(jnp.float32).reshape(count, -1, width)
    centered = pieces - jnp.mean(pieces, axis=-1, keepdims=True)
    variance = jnp.mean(centered * centered, axis=-1, keepdims=True)
    normed = (
        (centered * lax.rsqrt(variance + epsilon) * merge_gain)
        .reshape(count, -1)
        .astype(jnp.bfloat16)
    )
    inner = jax.nn.gelu(
        jnp.dot(normed, merge_first, preferred_element_type=jnp.float32), approximate=False
    ).astype(jnp.bfloat16)
    partial_merge = jnp.dot(inner, merge_second, preferred_element_type=jnp.float32)
    merged_full = lax.psum(partial_merge, ("blk", "mp")).astype(jnp.bfloat16)
    merged_mine = lax.dynamic_slice_in_dim(merged_full, model_index * slice_width, slice_width, 1)
    visual_all = lax.all_gather(merged_mine, "section", axis=0, tiled=True)
    query_full, keyval_full, out_full = (
        lax.all_gather(query_weight, "blk", axis=1, tiled=True),
        lax.all_gather(keyval_weight, "blk", axis=1, tiled=True),
        lax.all_gather(out_weight, "blk", axis=2, tiled=True),
    )
    query_full = query_full[0]
    kv_heads = keyval_full.shape[2]
    head_size = keyval_full.shape[4]
    keyval_full = keyval_full[0].reshape(keyval_full.shape[1], -1)
    out_full = out_full[0]
    gain_here = norm_gain[0]
    group = query_full.shape[1] // (kv_heads * head_size)
    scale = 1.0 / head_size**0.5
    key_where = jnp.arange(seq_len)
    ticks = blocks + lax.axis_size("section") - 1
    zero_index = jnp.zeros((), jnp.int32)
    held = jnp.zeros((rows_here, slice_width), jnp.bfloat16)
    cache_keys = jnp.zeros((seq_len, kv_heads, head_size), jnp.bfloat16)
    cache_values = jnp.zeros((seq_len, kv_heads, head_size), jnp.bfloat16)
    outputs = jnp.zeros((blocks, rows_here, slice_width), jnp.bfloat16)
    for tick_now in range(ticks):
        bound = min(tick_now + 1, blocks) * block_len
        block_now = tick_now - section_index
        active = (block_now >= 0) & (block_now < blocks)
        block_safe = jnp.clip(block_now, 0, blocks - 1)
        row_where = block_safe * block_len + cycle_index * rows_here + jnp.arange(rows_here)
        is_visual = positions[None, :] == row_where[:, None]
        picked = jnp.dot(
            is_visual.astype(jnp.bfloat16), visual_all, preferred_element_type=jnp.float32
        ).astype(jnp.bfloat16)
        text_rows = lax.dynamic_index_in_dim(text_embeds, block_safe, 0, keepdims=False)
        embedded = jnp.where(jnp.any(is_visual, axis=1)[:, None], picked, text_rows)
        incoming = jnp.where(section_index == 0, embedded, held)
        features = lax.all_gather(incoming, "mp", axis=1, tiled=True)
        feat_f = features.astype(jnp.float32)
        normx = (
            feat_f
            * lax.rsqrt(jnp.mean(feat_f * feat_f, axis=-1, keepdims=True) + epsilon)
            * gain_here
        ).astype(jnp.bfloat16)
        cosine, sine = rope_tables(row_where, head_size)
        query = jnp.dot(normx, query_full, preferred_element_type=jnp.float32).reshape(
            rows_here, -1, head_size
        )
        query = (
            rotate(query, cosine, sine)
            .astype(jnp.bfloat16)
            .reshape(rows_here, kv_heads, group, head_size)
        )
        keyval = jnp.dot(normx, keyval_full, preferred_element_type=jnp.float32).reshape(
            rows_here, kv_heads, 2, head_size
        )
        new_keys = rotate(keyval[:, :, 0, :], cosine, sine).astype(jnp.bfloat16)
        new_values = keyval[:, :, 1, :].astype(jnp.bfloat16)
        block_keys, block_values = (
            lax.all_gather(new_keys, "blk", axis=0, tiled=True),
            lax.all_gather(new_values, "blk", axis=0, tiled=True),
        )
        start = block_safe * block_len
        cache_keys = jnp.where(
            active,
            lax.dynamic_update_slice(cache_keys, block_keys, (start, zero_index, zero_index)),
            cache_keys,
        )
        cache_values = jnp.where(
            active,
            lax.dynamic_update_slice(cache_values, block_values, (start, zero_index, zero_index)),
            cache_values,
        )
        keys_seen = cache_keys[:bound]
        values_seen = cache_values[:bound]
        scores = (
            jnp.einsum("qkgd,skd->kgqs", query, keys_seen, preferred_element_type=jnp.float32)
            * scale
        )
        row_segments = jnp.take(segments, row_where)
        allowed = (key_where[None, :bound] <= row_where[:, None]) & (
            segments[None, :bound] == row_segments[:, None]
        )
        scores = jnp.where(allowed[None, None], scores, -jnp.inf)
        top = jnp.max(scores, axis=-1, keepdims=True)
        expo = jnp.exp(scores - top)
        probs = (expo / jnp.sum(expo, axis=-1, keepdims=True)).astype(jnp.bfloat16)
        attended = jnp.einsum(
            "kgqs,skd->qkgd", probs, values_seen, preferred_element_type=jnp.float32
        )
        attended = attended.reshape(rows_here, -1).astype(jnp.bfloat16)
        term = jnp.dot(attended, out_full, preferred_element_type=jnp.float32)
        summed = lax.psum_scatter(
            term.astype(jnp.bfloat16), "mp", scatter_dimension=1, tiled=True
        ).astype(jnp.float32)
        result = (incoming.astype(jnp.float32) + summed).astype(jnp.bfloat16)
        outputs = jnp.where(
            active,
            lax.dynamic_update_slice(outputs, result[None], (block_safe, zero_index, zero_index)),
            outputs,
        )
        held = shifted(result, "section", 1)
    return outputs[None]


def solution(mesh):
    return jax.shard_map(
        local,
        mesh=mesh,
        in_specs=(
            P("section", None),
            P(),
            P(None, ("blk", "mp")),
            P(("blk", "mp"), None),
            P(None, "blk", "mp"),
            P(),
            P(),
            P("section", None),
            P("section", "blk", "mp"),
            P("section", "blk", "mp", None, None),
            P("section", "mp", "blk"),
        ),
        out_specs=P("section", None, "blk", "mp"),
        check_vma=False,
    )
```

profile of v0, /device:TPU:0, one launch (start us, length us, event | category | flops | bytes accessed | tf_op | source)
XLA Modules:
  0.0 577.3 jit_solution(15734993620691398632)
XLA Ops:
  23.1 8.2 %fusion.130 = f32[128,4096]{1,0:T(8,128)} fusion(bf16[320,4096]{1,0:T(8,128)(2,1)} %param.16, bf16[5120,320]{0,1:T(8,128)(2,1)S(1)} %copy-done, f32[128,5120]{1,0:T(8,128)} %bitcast.320, f32[128,5120]{1,0:T(8,128)} %bitcast.321, f32[5120]{0:T(1024)S(1)} %mul.588, bf16[128,5120]{1,0:T(8,128)(2,1)} %param.13), kind=kOutput, calls=%fused_computation.172 | convolution fusion | flops 760913920 | bytes 14569472 | tf_op jit(solution)/shard_map/dot_general | solution.py:68
  31.4 111.0 %all-reduce.1 = bf16[128,4096]{1,0:T(8,128)(2,1)S(1)} all-reduce(f32[128,4096]{1,0:T(8,128)} %fusion.130), channel_id=1, replica_groups=mesh['section'=2,'blk'=4,'mp'=4] {'blk','mp'}, use_global_device_ids=true, to_apply=%region_3.4 | all-reduce | flops 524288 | bytes 3145728 | tf_op jit(solution)/shard_map/psum | solution.py:69
  147.9 16.1 %all_gather.58 = bf16[64,4096]{1,0:T(8,128)(2,1)S(1)} all-gather(bf16[64,1024]{1,0:T(8,128)(2,1)S(1)} %fusion.45), channel_id=1, replica_groups=mesh['section'=2,'blk'=4,'mp'=4] {'mp'}, dimensions={1}, use_global_device_ids=true | all-gather | bytes 655360 | tf_op jit(solution)/shard_map/all_gather | solution.py:105
  171.3 7.9 %all_gather.61 = bf16[256,1,128]{2,0,1:T(8,128)(2,1)S(1)} all-gather(bf16[64,1,128]{2,0,1:T(8,128)(2,1)S(1)} %pad_maximum_fusion), channel_id=1, replica_groups=mesh['section'=2,'blk'=4,'mp'=4] {'blk'}, dimensions={0}, use_global_device_ids=true | all-gather | bytes 81920 | tf_op jit(solution)/shard_map/all_gather | solution.py:127
  179.3 8.1 %all-gather = bf16[256,1,1,128]{3,0,2,1:T(8,128)(2,1)S(1)} all-gather(bf16[64,1,1,128]{3,0,2,1:T(8,128)(2,1)S(1)} %slice.285), channel_id=2, replica_groups=mesh['section'=2,'blk'=4,'mp'=4] {'blk'}, dimensions={0}, use_global_device_ids=true | all-gather | bytes 81920 | tf_op jit(solution)/shard_map/all_gather | solution.py:128
  188.9 11.7 %copy.23 = bf16[1024,4096]{1,0:T(8,128)(2,1)} copy(bf16[1024,4096]{0,1:T(8,128)(2,1)} %bitcast.324) | data formatting | bytes 16777216 | tf_op jit(solution)/shard_map/dot_general | solution.py:113
  208.7 50.6 %all-gather.13.cloned.1.call-done = bf16[1,1024,4096]{2,1,0:T(8,128)(2,1)} async-done(((bf16[1,1024,1024]{2,1,0:T(8,128)(2,1)}), bf16[1,1024,4096]{2,1,0:T(8,128)(2,1)}) %all-gather.13.cloned.1.call-update) | async-done | bytes 8388624 | tf_op jit(solution)/shard_map/all_gather | solution.py:75
  266.5 20.4 %reduce-scatter.6.cloned.1.call-done = bf16[64,1024]{1,0:T(8,128)(2,1)} async-done(((bf16[64,4096]{1,0:T(8,128)(2,1)}), bf16[64,1024]{1,0:T(8,128)(2,1)}) %reduce-scatter.6.cloned.1.call-update) | async-done | bytes 131088 | tf_op jit(solution)/shard_map/reduce_scatter | solution.py:160
  292.1 16.1 %all_gather.64 = bf16[64,4096]{1,0:T(8,128)(2,1)S(1)} all-gather(bf16[64,1024]{1,0:T(8,128)(2,1)S(1)} %fusion.47), channel_id=1, replica_groups=mesh['section'=2,'blk'=4,'mp'=4] {'mp'}, dimensions={1}, use_global_device_ids=true | all-gather | bytes 655360 | tf_op jit(solution)/shard_map/all_gather | solution.py:105
  315.8 8.1 %all-gather.1 = bf16[256,1,1,128]{3,0,2,1:T(8,128)(2,1)S(1)} all-gather(bf16[64,1,1,128]{3,0,2,1:T(8,128)(2,1)S(1)} %slice.284), channel_id=3, replica_groups=mesh['section'=2,'blk'=4,'mp'=4] {'blk'}, dimensions={0}, use_global_device_ids=true | all-gather | bytes 81920 | tf_op jit(solution)/shard_map/all_gather | solution.py:128
  324.2 8.2 %all_gather.66 = bf16[256,1,128]{2,0,1:T(8,128)(2,1)S(1)} all-gather(bf16[64,1,128]{2,0,1:T(8,128)(2,1)S(1)} %pad_maximum_fusion.1), channel_id=1, replica_groups=mesh['section'=2,'blk'=4,'mp'=4] {'blk'}, dimensions={0}, use_global_device_ids=true | all-gather | bytes 81920 | tf_op jit(solution)/shard_map/all_gather | solution.py:127
  340.7 17.2 %reduce-scatter.8.cloned.1.call-done = bf16[64,1024]{1,0:T(8,128)(2,1)} async-done(((bf16[64,4096]{1,0:T(8,128)(2,1)}), bf16[64,1024]{1,0:T(8,128)(2,1)}) %reduce-scatter.8.cloned.1.call-update) | async-done | bytes 131088 | tf_op jit(solution)/shard_map/reduce_scatter | solution.py:160
  362.6 16.3 %all_gather.67 = bf16[64,4096]{1,0:T(8,128)(2,1)S(1)} all-gather(bf16[64,1024]{1,0:T(8,128)(2,1)S(1)} %broadcast_select_fusion.2), channel_id=1, replica_groups=mesh['section'=2,'blk'=4,'mp'=4] {'mp'}, dimensions={1}, use_global_device_ids=true | all-gather | bytes 655360 | tf_op jit(solution)/shard_map/all_gather | solution.py:105
  386.1 8.2 %all-gather.2 = bf16[256,1,1,128]{3,0,2,1:T(8,128)(2,1)S(1)} all-gather(bf16[64,1,1,128]{3,0,2,1:T(8,128)(2,1)S(1)} %slice.283), channel_id=4, replica_groups=mesh['section'=2,'blk'=4,'mp'=4] {'blk'}, dimensions={0}, use_global_device_ids=true | all-gather | bytes 81920 | tf_op jit(solution)/shard_map/all_gather | solution.py:128
  394.6 8.1 %all_gather.69 = bf16[256,1,128]{2,0,1:T(8,128)(2,1)S(1)} all-gather(bf16[64,1,128]{2,0,1:T(8,128)(2,1)S(1)} %pad_maximum_fusion.2), channel_id=1, replica_groups=mesh['section'=2,'blk'=4,'mp'=4] {'blk'}, dimensions={0}, use_global_device_ids=true | all-gather | bytes 81920 | tf_op jit(solution)/shard_map/all_gather | solution.py:127
  412.9 15.8 %reduce-scatter.10.cloned.1.call-done = bf16[64,1024]{1,0:T(8,128)(2,1)} async-done(((bf16[64,4096]{1,0:T(8,128)(2,1)}), bf16[64,1024]{1,0:T(8,128)(2,1)}) %reduce-scatter.10.cloned.1.call-update) | async-done | bytes 131088 | tf_op jit(solution)/shard_map/reduce_scatter | solution.py:160
  432.9 15.9 %all_gather.70 = bf16[64,4096]{1,0:T(8,128)(2,1)S(1)} all-gather(bf16[64,1024]{1,0:T(8,128)(2,1)S(1)} %broadcast_select_fusion.1), channel_id=1, replica_groups=mesh['section'=2,'blk'=4,'mp'=4] {'mp'}, dimensions={1}, use_global_device_ids=true | all-gather | bytes 655360 | tf_op jit(solution)/shard_map/all_gather | solution.py:105
  456.1 8.2 %all-gather.3 = bf16[256,1,1,128]{3,0,2,1:T(8,128)(2,1)S(1)} all-gather(bf16[64,1,1,128]{3,0,2,1:T(8,128)(2,1)S(1)} %slice.282), channel_id=5, replica_groups=mesh['section'=2,'blk'=4,'mp'=4] {'blk'}, dimensions={0}, use_global_device_ids=true | all-gather | bytes 81920 | tf_op jit(solution)/shard_map/all_gather | solution.py:128
  464.6 8.4 %all_gather.72 = bf16[256,1,128]{2,0,1:T(8,128)(2,1)S(1)} all-gather(bf16[64,1,128]{2,0,1:T(8,128)(2,1)S(1)} %pad_maximum_fusion.3), channel_id=1, replica_groups=mesh['section'=2,'blk'=4,'mp'=4] {'blk'}, dimensions={0}, use_global_device_ids=true | all-gather | bytes 81920 | tf_op jit(solution)/shard_map/all_gather | solution.py:127
  480.1 19.1 %reduce-scatter.12.cloned.1.call-done = bf16[64,1024]{1,0:T(8,128)(2,1)} async-done(((bf16[64,4096]{1,0:T(8,128)(2,1)}), bf16[64,1024]{1,0:T(8,128)(2,1)}) %reduce-scatter.12.cloned.1.call-update) | async-done | bytes 131088 | tf_op jit(solution)/shard_map/reduce_scatter | solution.py:160
  503.8 15.8 %all_gather.73 = bf16[64,4096]{1,0:T(8,128)(2,1)S(1)} all-gather(bf16[64,1024]{1,0:T(8,128)(2,1)S(1)} %broadcast_select_fusion), channel_id=1, replica_groups=mesh['section'=2,'blk'=4,'mp'=4] {'mp'}, dimensions={1}, use_global_device_ids=true | all-gather | bytes 655360 | tf_op jit(solution)/shard_map/all_gather | solution.py:105
  526.9 8.3 %all-gather.4 = bf16[256,1,1,128]{3,0,2,1:T(8,128)(2,1)S(1)} all-gather(bf16[64,1,1,128]{3,0,2,1:T(8,128)(2,1)S(1)} %slice.281), channel_id=6, replica_groups=mesh['section'=2,'blk'=4,'mp'=4] {'blk'}, dimensions={0}, use_global_device_ids=true | all-gather | bytes 81920 | tf_op jit(solution)/shard_map/all_gather | solution.py:128
  535.4 8.0 %all_gather.75 = bf16[256,1,128]{2,0,1:T(8,128)(2,1)S(1)} all-gather(bf16[64,1,128]{2,0,1:T(8,128)(2,1)S(1)} %pad_maximum_fusion.4), channel_id=1, replica_groups=mesh['section'=2,'blk'=4,'mp'=4] {'blk'}, dimensions={0}, use_global_device_ids=true | all-gather | bytes 81920 | tf_op jit(solution)/shard_map/all_gather | solution.py:127
  551.0 17.3 %reduce-scatter.14.cloned.1.call-done = bf16[64,1024]{1,0:T(8,128)(2,1)} async-done(((bf16[64,4096]{1,0:T(8,128)(2,1)}), bf16[64,1024]{1,0:T(8,128)(2,1)}) %reduce-scatter.14.cloned.1.call-update) | async-done | bytes 131088 | tf_op jit(solution)/shard_map/reduce_scatter | solution.py:160
  (287 shorter events, 128.8 us)
Async XLA Ops:
  6.5 159.0 %all-gather.9.cloned.1.call-start = ((), (), s32[]{:S(2)}) async-start(), calls=%async_computation.5 | async-start | bytes 2621440 | tf_op jit(solution)/shard_map/all_gather | solution.py:74
  7.3 181.6 %all-gather.11.cloned.1.call-start = ((), (), s32[]{:S(2)}) async-start(), calls=%async_computation.6 | async-start | bytes 10485760 | tf_op jit(solution)/shard_map/all_gather | solution.py:73
  8.0 251.3 %all-gather.13.cloned.1.call-start = ((), (), s32[]{:S(2)}) async-start(), calls=%async_computation.7 | async-start | bytes 10485760 | tf_op jit(solution)/shard_map/all_gather | solution.py:75
  8.8 278.2 %reduce-scatter.6.cloned.1.call-start = ((), (), s32[]{:S(2)}) async-start(), calls=%async_computation.8 | async-start | bytes 655360 | tf_op jit(solution)/shard_map/reduce_scatter | solution.py:160
  31.3 113.3 %copy-start.35 = (s32[64]{0:T(128)}, s32[64]{0:T(128)S(1)}, u32[]{:S(2)}) copy-start(s32[64]{0:T(128)S(1)} %iota_add_fusion.2) | copy-start | bytes 772
  31.3 132.9 %copy-start.37 = (f32[64]{0:T(128)}, f32[64]{0:T(128)S(1)}, u32[]{:S(2)}) copy-start(f32[64]{0:T(128)S(1)} %fusion.290) | copy-start | bytes 772
  31.3 132.9 %copy-start.33 = (f32[64]{0:T(128)}, f32[64]{0:T(128)S(1)}, u32[]{:S(2)}) copy-start(f32[64]{0:T(128)S(1)} %get-tuple-element.79) | copy-start | bytes 772
  31.3 132.9 %copy-start.29 = (f32[64]{0:T(128)}, f32[64]{0:T(128)S(1)}, u32[]{:S(2)}) copy-start(f32[64]{0:T(128)S(1)} %get-tuple-element.81) | copy-start | bytes 772
  31.4 132.9 %copy-start.31 = (f32[64]{0:T(128)}, f32[64]{0:T(128)S(1)}, u32[]{:S(2)}) copy-start(f32[64]{0:T(128)S(1)} %get-tuple-element.80) | copy-start | bytes 772
  31.4 113.2 %slice-start = ((s32[1024]{0:T(1024)}), s32[256]{0:T(256)S(1)}, s32[]{:S(2)}) async-start(s32[1024]{0:T(1024)} %param.19), calls=%async_computation.13 | async-start | bytes 2048 | tf_op jit(solution)/shard_map/slice | solution.py:149
  31.4 113.2 %copy-start.26 = (s32[256]{0:T(256)S(1)}, s32[256]{0:T(256)}, u32[]{:S(2)}) copy-start(s32[256]{0:T(256)} %param.18) | copy-start | bytes 3076
  31.4 113.2 %slice-start.10 = ((s32[1024]{0:T(1024)}), s32[256]{0:T(256)S(1)}, s32[]{:S(2)}) async-start(s32[1024]{0:T(1024)} %copy-done.28), calls=%async_computation.23 | async-start | bytes 2048 | tf_op jit(solution)/shard_map/slice | solution.py:148
  265.1 92.8 %reduce-scatter.8.cloned.1.call-start = ((), (), s32[]{:S(2)}) async-start(), calls=%async_computation.9 | async-start | bytes 655360 | tf_op jit(solution)/shard_map/reduce_scatter | solution.py:160
  288.0 2.3 collective-permute-start
  308.4 27.8 %slice-start.2 = ((s8[8388608]{0:T(1024)(128)(4,1)}), s8[4194304]{0:T(1024)(128)(4,1)S(1)}, s32[]{:S(2)}) async-start(s8[8388608]{0:T(1024)(128)(4,1)} %bitcast.307), calls=%async_computation.15 | async-start | bytes 8388608
  309.3 27.0 %slice-start.3 = ((s8[8388608]{0:T(1024)(128)(4,1)}), s8[4194304]{0:T(1024)(128)(4,1)S(1)}, s32[]{:S(2)}) async-start(s8[8388608]{0:T(1024)(128)(4,1)} %bitcast.307), calls=%async_computation.16 | async-start | bytes 8388608
  338.7 89.9 %reduce-scatter.10.cloned.1.call-start = ((), (), s32[]{:S(2)}) async-start(), calls=%async_computation.10 | async-start | bytes 655360 | tf_op jit(solution)/shard_map/reduce_scatter | solution.py:160
  359.6 2.3 collective-permute-start.1
  379.9 27.1 %slice-start.4 = ((s8[8388608]{0:T(1024)(128)(4,1)}), s8[4194304]{0:T(1024)(128)(4,1)S(1)}, s32[]{:S(2)}) async-start(s8[8388608]{0:T(1024)(128)(4,1)} %bitcast.309), calls=%async_computation.17 | async-start | bytes 8388608
  409.5 89.8 %reduce-scatter.12.cloned.1.call-start = ((), (), s32[]{:S(2)}) async-start(), calls=%async_computation.11 | async-start | bytes 655360 | tf_op jit(solution)/shard_map/reduce_scatter | solution.py:160
  429.7 2.3 collective-permute-start.2
  449.9 27.7 %slice-start.6 = ((s8[8388608]{0:T(1024)(128)(4,1)}), s8[4194304]{0:T(1024)(128)(4,1)S(1)}, s32[]{:S(2)}) async-start(s8[8388608]{0:T(1024)(128)(4,1)} %bitcast.311), calls=%async_computation.19 | async-start | bytes 8388608
  480.0 88.3 %reduce-scatter.14.cloned.1.call-start = ((), (), s32[]{:S(2)}) async-start(), calls=%async_computation.12 | async-start | bytes 655360 | tf_op jit(solution)/shard_map/reduce_scatter | solution.py:160
  500.3 3.4 collective-permute-start.3
  (43 other events, 602.7 us)
Sparse Core Ops, SparseCore 0:
  9.2 41.5 all-gather.8
  52.6 117.5 all-gather.10
  172.0 87.2 all-gather.12
  265.3 21.6 reduce-scatter.5
  338.8 19.0 reduce-scatter.7
  409.6 19.0 reduce-scatter.9
  480.1 19.0 reduce-scatter.11
  549.3 19.0 reduce-scatter.13
where the time goes:
time: 586 us; the launch traced here: 577 us
  blocking collectives  275 us (47%)
  waiting for transfers between devices  145 us (25%)
  matrix products  73.5 us (13%)
  local copies, waits for them, and re-layouts  35.6 us (6%)
  other arithmetic  28 us (5%)
  between operations  15.3 us (3%)
    psum x1, blocking collectives, local(): merged_full = lax.psum(partial_merge, ('blk', 'mp')).astype(jnp.bfloat16)  111 us
    reduce_scatter x5, waiting for transfers between devices, local(): lax.psum_scatter(term.astype(jnp.bfloat16), 'mp', scatter_dimension=1, ti...  89.9 us
    all_gather x5, blocking collectives, local(): features = lax.all_gather(incoming, 'mp', axis=1, tiled=True)  80.3 us
    all_gather x1, waiting for transfers between devices, local(): lax.all_gather(out_weight, 'blk', axis=2, tiled=True)  50.6 us
    all_gather x5, blocking collectives, local(): lax.all_gather(new_values, 'blk', axis=0, tiled=True)  40.8 us
    all_gather x5, blocking collectives, local(): lax.all_gather(new_keys, 'blk', axis=0, tiled=True)  40.7 us
    dot_general x5, matrix products, local(): jnp.dot(normx, query_full, preferred_element_type=jnp.float32)  31.2 us
    dot_general x5, matrix products, local(): term = jnp.dot(attended, out_full, preferred_element_type=jnp.float32)  15.2 us
  transfers between devices with their start and end apart: 12, of which 9 were waited for; matrix products, arithmetic and copies ran while one was open for 11% of the time, Pallas kernels for 0%

commit v1 on v0

v1 whole, which is shorter than its diff:
```python
import jax
import jax.numpy as jnp
from jax import lax
from jax.sharding import PartitionSpec as P

epsilon = 1e-06
rope_base = 1000000.0
bf16 = jnp.bfloat16
f32 = jnp.float32


def other_section(value):
    return lax.ppermute(value, "section", [(0, 1), (1, 0)])


def rope_tables(where_at, head_size):
    steps_half = jnp.arange(head_size // 2).astype(f32)
    inverse = jnp.exp(-jnp.log(rope_base) * 2.0 * steps_half / head_size)
    angles = where_at.astype(f32)[:, None] * inverse[None, :]
    return (jnp.cos(angles)[:, None, :], jnp.sin(angles)[:, None, :])


def rotate(values, cosine, sine):
    half = values.shape[-1] // 2
    first = values[..., :half]
    second = values[..., half:]
    return jnp.concatenate(
        [first * cosine - second * sine, second * cosine + first * sine], axis=-1
    )


def local(
    patches,
    merge_gain,
    merge_first,
    merge_second,
    text_embeds,
    positions,
    segments,
    norm_gain,
    query_weight,
    keyval_weight,
    out_weight,
):
    count = patches.shape[0]
    width = merge_gain.shape[0]
    blocks, rows_here, slice_width = text_embeds.shape
    seq_len = segments.shape[0]
    block_len = seq_len // blocks
    nb = lax.axis_size("blk")
    half_rows = rows_here // 2
    mine = blocks * half_rows
    section = lax.axis_index("section")
    cycle = lax.axis_index("blk")
    depth = query_weight.shape[1]
    kv_heads = keyval_weight.shape[2]
    head_size = keyval_weight.shape[4]
    group = query_weight.shape[2] // (kv_heads * head_size)
    half_group = group // 2
    half_cols = kv_heads * half_group * head_size
    out_cols = out_weight.shape[2]

    def halves(value):
        pick = lambda i: lax.dynamic_index_in_dim(value, i, 2, keepdims=False)
        return pick(section), pick(1 - section)

    q_keep, q_send = halves(query_weight[0].reshape(depth, kv_heads, 2, half_group * head_size))
    kv_here = keyval_weight[0].reshape(depth, kv_heads * 2 * head_size)
    in_keep = jnp.concatenate([q_keep.reshape(depth, half_cols), kv_here], axis=1)
    in_send = jnp.concatenate([q_send.reshape(depth, half_cols), kv_here], axis=1)
    o_parts = out_weight[0].reshape(kv_heads, 2, half_group * head_size, out_cols)
    o_keep = lax.dynamic_index_in_dim(o_parts, section, 1, keepdims=False).reshape(-1, out_cols)
    o_send = lax.dynamic_index_in_dim(o_parts, 1 - section, 1, keepdims=False).reshape(-1, out_cols)
    in_other = other_section(in_send)
    o_other = other_section(o_send)
    gain_other = other_section(norm_gain)
    first_here = section == 0
    in_layers = [jnp.where(first_here, in_keep, in_other), jnp.where(first_here, in_other, in_keep)]
    o_layers = [jnp.where(first_here, o_keep, o_other), jnp.where(first_here, o_other, o_keep)]
    gains = [
        jnp.where(first_here, norm_gain, gain_other)[0],
        jnp.where(first_here, gain_other, norm_gain)[0],
    ]
    in_full = [lax.all_gather(w, "blk", axis=0, tiled=True) for w in in_layers]
    o_full = [lax.all_gather(w, "blk", axis=0) for w in o_layers]

    pieces = patches.reshape(count, -1, width)
    normed = []
    for i in range(pieces.shape[1]):
        piece = patches[:, i * width : (i + 1) * width].astype(f32)
        centered = piece - jnp.mean(piece, axis=-1, keepdims=True)
        variance = jnp.mean(centered * centered, axis=-1, keepdims=True)
        normed.append((centered * lax.rsqrt(variance + epsilon) * merge_gain).astype(bf16))
    normed = jnp.concatenate(normed, axis=1)
    inner = jax.nn.gelu(
        jnp.dot(normed, merge_first, preferred_element_type=f32), approximate=False
    ).astype(bf16)
    partial_merge = jnp.dot(inner, merge_second, preferred_element_type=f32).astype(bf16)
    merged = lax.psum_scatter(partial_merge, "mp", scatter_dimension=1, tiled=True)
    merged = lax.psum_scatter(merged, "blk", scatter_dimension=0, tiled=True)
    visual = lax.all_gather(merged, ("section", "blk"), axis=0, tiled=True)

    def at(half, cyc):
        inside = cyc * rows_here + half * half_rows + jnp.arange(half_rows)
        return (jnp.arange(blocks)[:, None] * block_len + inside[None, :]).reshape(-1)

    row_where = jnp.concatenate([at(0, cycle), at(1, cycle)])
    key_where = jnp.concatenate([at(h, c) for c in range(nb) for h in range(2)])
    seg_parts = segments.reshape(blocks, nb, 2, half_rows).transpose(1, 2, 0, 3).reshape(nb, -1)
    key_seg = seg_parts.reshape(-1)
    row_seg = lax.dynamic_index_in_dim(seg_parts, cycle, 0, keepdims=False)
    allowed = (key_where[None, :] <= row_where[:, None]) & (key_seg[None, :] == row_seg[:, None])
    cosine, sine = rope_tables(row_where, head_size)

    mine_where = at(section, cycle)
    is_visual = positions[None, :] == mine_where[:, None]
    picked = jnp.dot(is_visual.astype(bf16), visual, preferred_element_type=f32).astype(bf16)
    text = lax.dynamic_slice_in_dim(text_embeds, section * half_rows, half_rows, 1)
    hidden = jnp.where(
        jnp.any(is_visual, axis=1)[:, None], picked, text.reshape(mine, slice_width)
    )

    scale = 1.0 / head_size**0.5
    outs = []
    for layer in range(2):
        feat = lax.all_gather(hidden, "mp", axis=1, tiled=True).astype(f32)
        normx = (
            feat
            * lax.rsqrt(jnp.mean(feat * feat, axis=-1, keepdims=True) + epsilon)
            * gains[layer]
        ).astype(bf16)
        normx = lax.all_gather(normx, "section", axis=0, tiled=True)
        proj = jnp.dot(normx, in_full[layer], preferred_element_type=f32)
        rows = proj.shape[0]
        query = rotate(proj[:, :half_cols].reshape(rows, -1, head_size), cosine, sine)
        query = query.astype(bf16).reshape(rows, kv_heads, half_group, head_size)
        keyval = proj[:, half_cols:].reshape(rows, kv_heads, 2, head_size)
        keys = rotate(keyval[:, :, 0], cosine, sine).astype(bf16)
        keyval = jnp.concatenate([keys, keyval[:, :, 1].astype(bf16)], axis=-1)
        keyval = lax.all_gather(keyval.reshape(rows, -1), "blk", axis=0, tiled=True)
        keyval = keyval.reshape(-1, kv_heads, 2, head_size)
        scores = (
            jnp.einsum("qkgd,skd->kgqs", query, keyval[:, :, 0], preferred_element_type=f32)
            * scale
        )
        scores = jnp.where(allowed[None, None], scores, -jnp.inf)
        top = jnp.max(scores, axis=-1, keepdims=True)
        expo = jnp.exp(scores - top)
        probs = (expo / jnp.sum(expo, axis=-1, keepdims=True)).astype(bf16)
        attended = jnp.einsum(
            "kgqs,skd->qkgd", probs, keyval[:, :, 1], preferred_element_type=f32
        )
        attended = attended.reshape(rows, -1).astype(bf16)
        term = jnp.concatenate(
            [
                jnp.dot(attended, o_full[layer][c], preferred_element_type=f32).astype(bf16)
                for c in range(nb)
            ],
            axis=1,
        )
        term = lax.psum_scatter(term, "section", scatter_dimension=0, tiled=True)
        term = lax.psum_scatter(term, "mp", scatter_dimension=1, tiled=True)
        hidden = (hidden.astype(f32) + term.astype(f32)).astype(bf16)
        outs.append(hidden)
    keep = jnp.where(first_here, outs[0], outs[1])
    got = other_section(jnp.where(first_here, outs[1], outs[0]))
    low = jnp.where(first_here, keep, got).reshape(blocks, half_rows, slice_width)
    high = jnp.where(first_here, got, keep).reshape(blocks, half_rows, slice_width)
    return jnp.concatenate([low, high], axis=1)[None]


def solution(mesh):
    return jax.shard_map(
        local,
        mesh=mesh,
        in_specs=(
            P("section", None),
            P(),
            P(None, ("blk", "mp")),
            P(("blk", "mp"), None),
            P(None, "blk", "mp"),
            P(),
            P(),
            P("section", None),
            P("section", "blk", "mp"),
            P("section", "blk", "mp", None, None),
            P("section", "mp", "blk"),
        ),
        out_specs=P("section", None, "blk", "mp"),
        check_vma=False,
    )
```

time: 586 us -> 548 us (0.935); the launches traced: 577 us -> 548 us
  waiting for transfers between devices: 145 us -> 402 us
  blocking collectives: 275 us -> 53.9 us
  matrix products: 73.5 us -> 31.2 us
  local copies, waits for them, and re-layouts: 35.6 us -> 13.7 us
    all_gather x3 -> x8, waiting for transfers between devices: 50.6 us -> 258 us  [the longest x2 129 us: local(): in_full = [lax.all_gather(w, 'blk', axis=0, tiled=True) for w in in_layers]]
    psum x1 -> x0, blocking collectives: 111 us -> none  [local(): merged_full = lax.psum(partial_merge, ('blk', 'mp')).astype(jnp.bfloat16)]
    all_gather x16 -> x3, blocking collectives: 164 us -> 53.9 us  [the longest x2 29.1 us: local(): keyval = lax.all_gather(keyval.reshape(rows, -1), 'blk', axis=0, tiled=True)]
    reduce_scatter x5 -> x6, waiting for transfers between devices: 89.9 us -> 135 us  [the longest x2 61.3 us: local(): term = lax.psum_scatter(term, 'mp', scatter_dimension=1, tiled=True)]
    dot_general x31 -> x16, matrix products: 73.5 us -> 31.2 us  [the longest x2 10.4 us: local(): proj = jnp.dot(normx, in_full[layer], preferred_element_type=f32)]
    dot_general x1 -> x0, local copies, waits for them, and re-layouts: 11.7 us -> none  [local(): jnp.dot(normx, query_full, preferred_element_type=jnp.float32)]
    convert_element_type x3 -> x5, other arithmetic: 0.02 us -> 9.54 us  [the longest x2 5.06 us: local(): normx = (feat * lax.rsqrt(jnp.mean(feat * feat, axis=-1, keepdims=True) +...]
    select_n x26 -> x5, other arithmetic: 14.2 us -> 7.33 us  [the longest x1 3.64 us: local(): jnp.where(first_here, in_other, in_keep)]
  transfers between devices with their start and end apart: 12 -> 18, of which waited for: 9 -> 16; matrix products, arithmetic and copies ran while one was open for 11% -> 8% of each run, Pallas kernels for 0% -> 0%
where the time goes in v1:
time: 548 us
  waiting for transfers between devices  402 us (73%)
  blocking collectives  53.9 us (10%)
  other arithmetic  32.6 us (6%)
  matrix products  31.2 us (6%)
  between operations  14 us (3%)
  local copies, waits for them, and re-layouts  13.7 us (2%)
    all_gather x2, waiting for transfers between devices, local(): in_full = [lax.all_gather(w, 'blk', axis=0, tiled=True) for w in in_layers]  129 us
    all_gather x2, waiting for transfers between devices, local(): o_full = [lax.all_gather(w, 'blk', axis=0) for w in o_layers]  65.5 us
    reduce_scatter x2, waiting for transfers between devices, local(): term = lax.psum_scatter(term, 'mp', scatter_dimension=1, tiled=True)  61.3 us
    all_gather x2, waiting for transfers between devices, local(): feat = lax.all_gather(hidden, 'mp', axis=1, tiled=True).astype(f32)  51 us
    reduce_scatter x1, waiting for transfers between devices, local(): lax.psum_scatter(partial_merge, 'mp', scatter_dimension=1, tiled=True)  29.9 us
    all_gather x2, blocking collectives, local(): keyval = lax.all_gather(keyval.reshape(rows, -1), 'blk', axis=0, tiled=True)  29.1 us
    all_gather x1, blocking collectives, local(): visual = lax.all_gather(merged, ('section', 'blk'), axis=0, tiled=True)  24.8 us
    reduce_scatter x1, waiting for transfers between devices, local(): merged = lax.psum_scatter(merged, 'blk', scatter_dimension=0, tiled=True)  24.4 us
  transfers between devices with their start and end apart: 18, of which 16 were waited for; matrix products, arithmetic and copies ran while one was open for 8% of the time, Pallas kernels for 0%

profile of v1, /device:TPU:0, one launch (start us, length us, event | category | flops | bytes accessed | tf_op | source)
XLA Modules:
  0.0 547.8 jit_solution(17795653030389927400)
XLA Ops:
  10.0 2.8 fusion.56
  12.8 6.2 %convolution_convert_fusion = bf16[128,4096]{1,0:T(8,128)(2,1)} fusion(bf16[320,4096]{1,0:T(8,128)(2,1)} %param.14, bf16[5120,320]{0,1:T(8,128)(2,1)S(1)} %copy-done, bf16[128,1280]{1,0:T(8,128)(2,1)} %get-tuple-element.22, bf16[128,1280]{1,0:T(8,128)(2,1)} %get-tuple-element.21, bf16[128,1280]{1,0:T(8,128)(2,1)} %get-tuple-element.20, ...), kind=kOutput, calls=%fused_computation | convolution fusion | flops 763404288 | bytes 8257536 | tf_op jit(solution)/shard_map/dot_general | solution.py:98
  19.2 29.9 %reduce-scatter.7.cloned.1.call-done = bf16[128,1024]{1,0:T(8,128)(2,1)} async-done(((bf16[128,4096]{1,0:T(8,128)(2,1)}), bf16[128,1024]{1,0:T(8,128)(2,1)}) %reduce-scatter.7.cloned.1.call-update) | async-done | bytes 262160 | tf_op jit(solution)/shard_map/reduce_scatter | solution.py:99
  50.4 24.4 %reduce-scatter.9.cloned.1.call-done = bf16[32,1024]{1,0:T(8,128)(2,1)} async-done(((bf16[128,1024]{1,0:T(8,128)(2,1)}), bf16[32,1024]{1,0:T(8,128)(2,1)}) %reduce-scatter.9.cloned.1.call-update) | async-done | bytes 65552 | tf_op jit(solution)/shard_map/reduce_scatter | solution.py:100
  74.8 24.8 %all_gather.39 = bf16[256,1024]{1,0:T(8,128)(2,1)S(1)} all-gather(bf16[32,1024]{1,0:T(8,128)(2,1)} %reduce-scatter.9.cloned.1.call-done), channel_id=1, replica_groups=mesh['section'=2,'blk'=4,'mp'=4] {'section','blk'}, dimensions={0}, use_global_device_ids=true | all-gather | bytes 589824 | tf_op jit(solution)/shard_map/all_gather | solution.py:101
  100.8 2.9 copy.75
  103.7 24.9 %all-gather.13.cloned.1.call-done = bf16[128,4096]{1,0:T(8,128)(2,1)} async-done(((bf16[128,1024]{1,0:T(8,128)(2,1)}), bf16[128,4096]{1,0:T(8,128)(2,1)}) %all-gather.13.cloned.1.call-update) | async-done | bytes 1048592 | tf_op jit(solution)/shard_map/all_gather | solution.py:126
  130.1 2.5 fusion.6
  138.4 3.2 collective-permute-done.1
  141.6 3.6 broadcast_select_fusion
  153.3 62.8 %all-gather.17.cloned.1.call-done = bf16[4096,768]{1,0:T(8,128)(2,1)} async-done(((bf16[1024,768]{1,0:T(8,128)(2,1)}), bf16[4096,768]{1,0:T(8,128)(2,1)}) %all-gather.17.cloned.1.call-update) | async-done | bytes 6291472 | tf_op jit(solution)/shard_map/all_gather | solution.py:84
  216.0 5.2 fusion.170
  222.3 14.7 %all-gather = bf16[1024,1,256]{2,0,1:T(8,128)(2,1)S(1)} all-gather(bf16[256,1,256]{2,0,1:T(8,128)(2,1)S(1)} %pad_maximum_fusion.4), channel_id=2, replica_groups=mesh['section'=2,'blk'=4,'mp'=4] {'blk'}, dimensions={0}, use_global_device_ids=true | all-gather | bytes 655360 | tf_op jit(solution)/shard_map/all_gather | solution.py:140
  241.1 32.1 %all-gather.25.cloned.1.call-done = bf16[2048,1024]{1,0:T(8,128)(2,1)} async-done(((bf16[512,1024]{1,0:T(8,128)(2,1)}), bf16[2048,1024]{1,0:T(8,128)(2,1)}) %all-gather.25.cloned.1.call-update) | async-done | bytes 4194320 | tf_op jit(solution)/shard_map/all_gather | solution.py:85
  279.4 9.7 %reduce-scatter.11.cloned.1.call-done = bf16[128,4096]{1,0:T(8,128)(2,1)} async-done(((bf16[256,4096]{1,0:T(8,128)(2,1)}), bf16[128,4096]{1,0:T(8,128)(2,1)}) %reduce-scatter.11.cloned.1.call-update) | async-done | bytes 1048592 | tf_op jit(solution)/shard_map/reduce_scatter | solution.py:161
  289.1 30.7 %reduce-scatter.13.cloned.1.call-done = bf16[128,1024]{1,0:T(8,128)(2,1)} async-done(((bf16[128,4096]{1,0:T(8,128)(2,1)}), bf16[128,1024]{1,0:T(8,128)(2,1)}) %reduce-scatter.13.cloned.1.call-update) | async-done | bytes 262160 | tf_op jit(solution)/shard_map/reduce_scatter | solution.py:162
  322.2 26.1 %all-gather.19.cloned.1.call-done = bf16[128,4096]{1,0:T(8,128)(2,1)} async-done(((bf16[128,1024]{1,0:T(8,128)(2,1)}), bf16[128,4096]{1,0:T(8,128)(2,1)}) %all-gather.19.cloned.1.call-update) | async-done | bytes 1048592 | tf_op jit(solution)/shard_map/all_gather | solution.py:126
  353.0 66.7 %all-gather.23.cloned.1.call-done = bf16[4096,768]{1,0:T(8,128)(2,1)} async-done(((bf16[1024,768]{1,0:T(8,128)(2,1)}), bf16[4096,768]{1,0:T(8,128)(2,1)}) %all-gather.23.cloned.1.call-update) | async-done | bytes 6291472 | tf_op jit(solution)/shard_map/all_gather | solution.py:84
  419.7 12.2 %all-gather.21.cloned.1.call-done = bf16[256,4096]{1,0:T(8,128)(2,1)} async-done(((bf16[128,4096]{1,0:T(8,128)(2,1)}), bf16[256,4096]{1,0:T(8,128)(2,1)}) %all-gather.21.cloned.1.call-update) | async-done | bytes 2097168 | tf_op jit(solution)/shard_map/all_gather | solution.py:132
  431.8 5.2 fusion.171
  438.1 14.5 %all-gather.2 = bf16[1024,1,256]{2,0,1:T(8,128)(2,1)S(1)} all-gather(bf16[256,1,256]{2,0,1:T(8,128)(2,1)S(1)} %pad_maximum_fusion.5), channel_id=4, replica_groups=mesh['section'=2,'blk'=4,'mp'=4] {'blk'}, dimensions={0}, use_global_device_ids=true | all-gather | bytes 655360 | tf_op jit(solution)/shard_map/all_gather | solution.py:140
  456.9 33.4 %all-gather.27.cloned.1.call-done = bf16[2048,1024]{1,0:T(8,128)(2,1)} async-done(((bf16[512,1024]{1,0:T(8,128)(2,1)}), bf16[2048,1024]{1,0:T(8,128)(2,1)}) %all-gather.27.cloned.1.call-update) | async-done | bytes 4194320 | tf_op jit(solution)/shard_map/all_gather | solution.py:85
  496.4 9.7 %reduce-scatter.15.cloned.1.call-done = bf16[128,4096]{1,0:T(8,128)(2,1)} async-done(((bf16[256,4096]{1,0:T(8,128)(2,1)}), bf16[128,4096]{1,0:T(8,128)(2,1)}) %reduce-scatter.15.cloned.1.call-update) | async-done | bytes 1048592 | tf_op jit(solution)/shard_map/reduce_scatter | solution.py:161
  506.1 30.6 %reduce-scatter.17.cloned.1.call-done = bf16[128,1024]{1,0:T(8,128)(2,1)} async-done(((bf16[128,4096]{1,0:T(8,128)(2,1)}), bf16[128,1024]{1,0:T(8,128)(2,1)}) %reduce-scatter.17.cloned.1.call-update) | async-done | bytes 262160 | tf_op jit(solution)/shard_map/reduce_scatter | solution.py:162
  (169 shorter events, 55.3 us)
Async XLA Ops:
  6.5 6.3 %copy-start = (bf16[5120,320]{0,1:T(8,128)(2,1)S(1)}, bf16[5120,320]{0,1:T(8,128)(2,1)}, u32[]{:S(2)}) copy-start(bf16[5120,320]{0,1:T(8,128)(2,1)} %param.13) | copy-start | bytes 9830404
  6.5 42.5 %reduce-scatter.7.cloned.1.call-start = ((), (), s32[]{:S(2)}) async-start(), calls=%async_computation.6 | async-start | bytes 1310720 | tf_op jit(solution)/shard_map/reduce_scatter | solution.py:99
  12.8 36.5 %copy-start.7 = (s32[256]{0:T(256)S(1)}, s32[256]{0:T(256)}, u32[]{:S(2)}) copy-start(s32[256]{0:T(256)} %param.16) | copy-start | bytes 3076
  12.8 87.8 %copy-start.5 = (f32[1,4096]{1,0:T(1,128)S(1)}, f32[1,4096]{1,0:T(1,128)}, u32[]{:S(2)}) copy-start(f32[1,4096]{1,0:T(1,128)} %param.18) | copy-start | bytes 49156
  19.1 55.7 %reduce-scatter.9.cloned.1.call-start = ((), (), s32[]{:S(2)}) async-start(), calls=%async_computation.7 | async-start | bytes 327680 | tf_op jit(solution)/shard_map/reduce_scatter | solution.py:100
  49.1 79.5 %all-gather.13.cloned.1.call-start = ((), (), s32[]{:S(2)}) async-start(), calls=%async_computation.8 | async-start | bytes 1310720 | tf_op jit(solution)/shard_map/all_gather | solution.py:126
  100.6 52.7 %all-gather.15.cloned.1.call-start = ((), (), s32[]{:S(2)}) async-start(), calls=%async_computation.9 | async-start | bytes 3145728 | tf_op jit(solution)/shard_map/all_gather | solution.py:132
  100.6 3.0 collective-permute-start
  132.7 83.3 %all-gather.17.cloned.1.call-start = ((), (), s32[]{:S(2)}) async-start(), calls=%async_computation.10 | async-start | bytes 7864320 | tf_op jit(solution)/shard_map/all_gather | solution.py:84
  137.8 3.8 collective-permute-start.1
  145.3 128.0 %all-gather.25.cloned.1.call-start = ((), (), s32[]{:S(2)}) async-start(), calls=%async_computation.18 | async-start | bytes 5242880 | tf_op jit(solution)/shard_map/all_gather | solution.py:85
  146.7 2.7 collective-permute-start.2
  151.0 138.0 %reduce-scatter.11.cloned.1.call-start = ((), (), s32[]{:S(2)}) async-start(), calls=%async_computation.11 | async-start | bytes 3145728 | tf_op jit(solution)/shard_map/reduce_scatter | solution.py:161
  277.8 42.1 %copy-start.3 = (bf16[128,1024]{1,0:T(8,128)(2,1)S(1)}, bf16[128,1024]{1,0:T(8,128)(2,1)}, u32[]{:S(2)}) copy-start(bf16[128,1024]{1,0:T(8,128)(2,1)} %fusion.28) | copy-start | bytes 786436
  279.3 40.5 %reduce-scatter.13.cloned.1.call-start = ((), (), s32[]{:S(2)}) async-start(), calls=%async_computation.12 | async-start | bytes 1310720 | tf_op jit(solution)/shard_map/reduce_scatter | solution.py:162
  289.1 59.2 %all-gather.19.cloned.1.call-start = ((), (), s32[]{:S(2)}) async-start(), calls=%async_computation.13 | async-start | bytes 1310720 | tf_op jit(solution)/shard_map/all_gather | solution.py:126
  321.6 98.1 %all-gather.23.cloned.1.call-start = ((), (), s32[]{:S(2)}) async-start(), calls=%async_computation.15 | async-start | bytes 7864320 | tf_op jit(solution)/shard_map/all_gather | solution.py:84
  322.2 109.7 %all-gather.21.cloned.1.call-start = ((), (), s32[]{:S(2)}) async-start(), calls=%async_computation.14 | async-start | bytes 3145728 | tf_op jit(solution)/shard_map/all_gather | solution.py:132
  352.4 137.9 %all-gather.27.cloned.1.call-start = ((), (), s32[]{:S(2)}) async-start(), calls=%async_computation.19 | async-start | bytes 5242880 | tf_op jit(solution)/shard_map/all_gather | solution.py:85
  353.0 153.1 %reduce-scatter.15.cloned.1.call-start = ((), (), s32[]{:S(2)}) async-start(), calls=%async_computation.16 | async-start | bytes 3145728 | tf_op jit(solution)/shard_map/reduce_scatter | solution.py:161
  494.7 41.9 %copy-start.2 = (bf16[128,1024]{1,0:T(8,128)(2,1)S(1)}, bf16[128,1024]{1,0:T(8,128)(2,1)}, u32[]{:S(2)}) copy-start(bf16[128,1024]{1,0:T(8,128)(2,1)} %add_convert_fusion.2) | copy-start | bytes 786436
  494.8 46.5 %copy-start.1 = (bf16[5120,320]{0,1:T(8,128)(2,1)S(1)}, bf16[5120,320]{0,1:T(8,128)(2,1)}, u32[]{:S(2)}) copy-start(bf16[5120,320]{0,1:T(8,128)(2,1)} %param.13) | copy-start | bytes 9830404
  496.3 40.4 %reduce-scatter.17.cloned.1.call-start = ((), (), s32[]{:S(2)}) async-start(), calls=%async_computation.17 | async-start | bytes 1310720 | tf_op jit(solution)/shard_map/reduce_scatter | solution.py:162
  537.7 1.6 collective-permute-start.3
  (4 other events, 17.2 us)
Sparse Core Ops, SparseCore 0:
  19.2 29.8 reduce-scatter.6
  52.0 22.7 reduce-scatter.8
  100.7 27.8 all-gather.12
  132.8 10.0 all-gather.14
  145.4 70.6 all-gather.16
  217.7 55.4 all-gather.24
  279.4 9.5 reduce-scatter.10
  291.4 28.3 reduce-scatter.12
  321.7 26.5 all-gather.18
  350.0 69.6 all-gather.22
  421.2 10.5 all-gather.20
  433.5 56.6 all-gather.26
  496.4 9.6 reduce-scatter.14
  508.3 28.3 reduce-scatter.16

commit v2 on v1

--- a/solution.py
+++ b/solution.py
@@ -11,6 +11,49 @@
 
 def other_section(value):
     return lax.ppermute(value, "section", [(0, 1), (1, 0)])
+
+
+def swap_blk(value, bit):
+    return lax.ppermute(value, "blk", [(i, i ^ bit) for i in range(lax.axis_size("blk"))])
+
+
+def near_blk(value):
+    half = value.shape[0] // 2
+    low, high = value[:half], value[half:]
+    if lax.axis_size("blk") != 4:
+        return (value,)
+    return low, high, swap_blk(low, 1), swap_blk(high, 2), swap_blk(low, 2), swap_blk(high, 1)
+
+
+def far_blk(near):
+    if len(near) == 1:
+        return (lax.all_gather(near[0], "blk", axis=0),)
+    return swap_blk(near[2], 2), swap_blk(near[3], 1)
+
+
+def blocks_of(near, far):
+    if len(near) == 1:
+        half = far[0].shape[1] // 2
+        return [(c, far[0][c, :half], far[0][c, half:]) for c in range(far[0].shape[0])]
+    cycle = lax.axis_index("blk")
+    low, high, low_1, high_2, low_2, high_1 = near
+    return [
+        (cycle, low, high),
+        (cycle ^ 1, low_1, high_1),
+        (cycle ^ 2, low_2, high_2),
+        (cycle ^ 3, far[0], far[1]),
+    ]
+
+
+def together(value, *moved):
+    return lax.optimization_barrier((value, *moved))
+
+
+def dot_halves(left, low, high):
+    half = low.shape[0]
+    return jnp.dot(left[:, :half], low, preferred_element_type=f32) + jnp.dot(
+        left[:, half:], high, preferred_element_type=f32
+    )
 
 
 def rope_tables(where_at, head_size):
@@ -81,8 +124,8 @@
         jnp.where(first_here, norm_gain, gain_other)[0],
         jnp.where(first_here, gain_other, norm_gain)[0],
     ]
-    in_full = [lax.all_gather(w, "blk", axis=0, tiled=True) for w in in_layers]
-    o_full = [lax.all_gather(w, "blk", axis=0) for w in o_layers]
+    in_near = near_blk(in_layers[0])
+    o_near = near_blk(o_layers[0])
 
     pieces = patches.reshape(count, -1, width)
     normed = []
@@ -97,18 +140,28 @@
     ).astype(bf16)
     partial_merge = jnp.dot(inner, merge_second, preferred_element_type=f32).astype(bf16)
     merged = lax.psum_scatter(partial_merge, "mp", scatter_dimension=1, tiled=True)
+    merged, in_near = together(merged, in_near)
+    in_far = far_blk(in_near)
     merged = lax.psum_scatter(merged, "blk", scatter_dimension=0, tiled=True)
     visual = lax.all_gather(merged, ("section", "blk"), axis=0, tiled=True)
+    visual, in_far, o_near = together(visual, in_far, o_near)
 
     def at(half, cyc):
         inside = cyc * rows_here + half * half_rows + jnp.arange(half_rows)
         return (jnp.arange(blocks)[:, None] * block_len + inside[None, :]).reshape(-1)
 
-    row_where = jnp.concatenate([at(0, cycle), at(1, cycle)])
-    key_where = jnp.concatenate([at(h, c) for c in range(nb) for h in range(2)])
-    seg_parts = segments.reshape(blocks, nb, 2, half_rows).transpose(1, 2, 0, 3).reshape(nb, -1)
-    key_seg = seg_parts.reshape(-1)
-    row_seg = lax.dynamic_index_in_dim(seg_parts, cycle, 0, keepdims=False)
+    sides = (section, 1 - section)
+    if nb == 4:
+        key_order = [cycle ^ k for k in range(nb)]
+    else:
+        key_order = list(range(nb))
+    seg_parts = segments.reshape(blocks, nb, 2, half_rows).transpose(1, 2, 0, 3)
+    seg_parts = seg_parts.reshape(nb * 2, -1)
+    seg_at = lambda h, c: lax.dynamic_index_in_dim(seg_parts, c * 2 + h, 0, keepdims=False)
+    row_where = jnp.concatenate([at(h, cycle) for h in sides])
+    row_seg = jnp.concatenate([seg_at(h, cycle) for h in sides])
+    key_where = jnp.concatenate([at(h, c) for c in key_order for h in sides])
+    key_seg = jnp.concatenate([seg_at(h, c) for c in key_order for h in sides])
     allowed = (key_where[None, :] <= row_where[:, None]) & (key_seg[None, :] == row_seg[:, None])
     cosine, sine = rope_tables(row_where, head_size)
 
@@ -123,21 +176,37 @@
     scale = 1.0 / head_size**0.5
     outs = []
     for layer in range(2):
-        feat = lax.all_gather(hidden, "mp", axis=1, tiled=True).astype(f32)
+        feat = lax.all_gather(hidden, "mp", axis=1, tiled=True)
+        if layer == 0:
+            o_far = far_blk(o_near)
+            feat, o_far = together(feat, o_far)
+            next_near = near_blk(in_layers[1])
+        else:
+            o_near = near_blk(o_layers[1])
+            feat, o_near = together(feat, o_near)
+            o_far = far_blk(o_near)
+        feat = feat.astype(f32)
         normx = (
             feat
             * lax.rsqrt(jnp.mean(feat * feat, axis=-1, keepdims=True) + epsilon)
             * gains[layer]
         ).astype(bf16)
-        normx = lax.all_gather(normx, "section", axis=0, tiled=True)
-        proj = jnp.dot(normx, in_full[layer], preferred_element_type=f32)
+        normx = jnp.concatenate([normx, other_section(normx)], axis=0)
+        proj = sum(
+            dot_halves(lax.dynamic_slice_in_dim(normx, c * depth, depth, 1), low, high)
+            for c, low, high in blocks_of(in_near, in_far)
+        )
         rows = proj.shape[0]
         query = rotate(proj[:, :half_cols].reshape(rows, -1, head_size), cosine, sine)
         query = query.astype(bf16).reshape(rows, kv_heads, half_group, head_size)
         keyval = proj[:, half_cols:].reshape(rows, kv_heads, 2, head_size)
         keys = rotate(keyval[:, :, 0], cosine, sine).astype(bf16)
         keyval = jnp.concatenate([keys, keyval[:, :, 1].astype(bf16)], axis=-1)
-        keyval = lax.all_gather(keyval.reshape(rows, -1), "blk", axis=0, tiled=True)
+        keyval = keyval.reshape(rows, -1)
+        if nb == 4:
+            keyval = jnp.concatenate([keyval] + [swap_blk(keyval, k) for k in (1, 2, 3)], axis=0)
+        else:
+            keyval = lax.all_gather(keyval, "blk", axis=0, tiled=True)
         keyval = keyval.reshape(-1, kv_heads, 2, head_size)
         scores = (
             jnp.einsum("qkgd,skd->kgqs", query, keyval[:, :, 0], preferred_element_type=f32)
@@ -151,16 +220,24 @@
             "kgqs,skd->qkgd", probs, keyval[:, :, 1], preferred_element_type=f32
         )
         attended = attended.reshape(rows, -1).astype(bf16)
-        term = jnp.concatenate(
-            [
-                jnp.dot(attended, o_full[layer][c], preferred_element_type=f32).astype(bf16)
-                for c in range(nb)
-            ],
-            axis=1,
-        )
-        term = lax.psum_scatter(term, "section", scatter_dimension=0, tiled=True)
+        if layer == 0:
+            attended, next_near = together(attended, next_near)
+            next_far = far_blk(next_near)
+
+        def terms(part):
+            whole = jnp.zeros((mine, nb * out_cols), bf16)
+            for c, low, high in blocks_of(o_near, o_far):
+                here = dot_halves(part, low, high).astype(bf16)
+                whole = lax.dynamic_update_slice_in_dim(whole, here, c * out_cols, 1)
+            return whole
+
+        theirs = other_section(terms(attended[mine:]))
+        term = (terms(attended[:mine]).astype(f32) + theirs.astype(f32)).astype(bf16)
         term = lax.psum_scatter(term, "mp", scatter_dimension=1, tiled=True)
         hidden = (hidden.astype(f32) + term.astype(f32)).astype(bf16)
+        if layer == 0:
+            hidden, in_far = together(hidden, next_far)
+            in_near = next_near
         outs.append(hidden)
     keep = jnp.where(first_here, outs[0], outs[1])
     got = other_section(jnp.where(first_here, outs[1], outs[0]))

time: 548 us -> 384 us (0.70)
  waiting for transfers between devices: 402 us -> 164 us
  starting transfers between devices: 0.99 us -> 36.9 us
  matrix products: 31.2 us -> 63.8 us
  local copies, waits for them, and re-layouts: 13.7 us -> 32.1 us
  blocking collectives: 53.9 us -> 37.7 us
    all_gather x8 -> x2, waiting for transfers between devices: 258 us -> 12.5 us  [local(): feat = lax.all_gather(hidden, 'mp', axis=1, tiled=True)]
    ppermute x0 -> x30, waiting for transfers between devices: none -> 75.5 us  [swap_blk(): lax.ppermute(value, 'blk', [(i, i ^ bit) for i in range(lax.axis_size('bl...]
    ppermute x0 -> x30, starting transfers between devices: none -> 35.6 us  [swap_blk(): lax.ppermute(value, 'blk', [(i, i ^ bit) for i in range(lax.axis_size('bl...]
    dot_general x10 -> x48, matrix products: 19.3 us -> 52.1 us  [the longest x24 27.4 us: dot_halves(): jnp.dot(left[:, half:], high, preferred_element_type=f32)]
    all_gather x2 -> x0, blocking collectives: 29.1 us -> none  [local(): keyval = lax.all_gather(keyval.reshape(rows, -1), 'blk', axis=0, tiled=True)]
    reduce_scatter x2 -> x0, waiting for transfers between devices: 19.4 us -> none  [local(): term = lax.psum_scatter(term, 'section', scatter_dimension=0, tiled=True)]
    reduce_scatter x1, waiting for transfers between devices: 29.9 us -> 11.7 us  [local(): lax.psum_scatter(partial_merge, 'mp', scatter_dimension=1, tiled=True)]
    all_gather x1, blocking collectives: 24.8 us -> 37.7 us  [local(): visual = lax.all_gather(merged, ('section', 'blk'), axis=0, tiled=True)]
  transfers between devices with their start and end apart: 18 -> 44, of which waited for: 16 -> 20; matrix products, arithmetic and copies ran while one was open for 8% -> 23% of each run, Pallas kernels for 0% -> 0%
where the time goes in v2:
time: 384 us; the launch traced here: 381 us
  waiting for transfers between devices  164 us (43%)
  matrix products  63.8 us (17%)
  blocking collectives  37.7 us (10%)
  starting transfers between devices  36.9 us (10%)
  local copies, waits for them, and re-layouts  32.1 us (8%)
  other arithmetic  31.7 us (8%)
  between operations  14.8 us (4%)
    ppermute x30, waiting for transfers between devices, swap_blk(): lax.ppermute(value, 'blk', [(i, i ^ bit) for i in range(lax.axis_size('bl...  75.5 us
    reduce_scatter x2, waiting for transfers between devices, local(): term = lax.psum_scatter(term, 'mp', scatter_dimension=1, tiled=True)  50.2 us
    all_gather x1, blocking collectives, local(): visual = lax.all_gather(merged, ('section', 'blk'), axis=0, tiled=True)  37.7 us
    ppermute x30, starting transfers between devices, swap_blk(): lax.ppermute(value, 'blk', [(i, i ^ bit) for i in range(lax.axis_size('bl...  35.6 us
    dot_general x24, matrix products, dot_halves(): jnp.dot(left[:, half:], high, preferred_element_type=f32)  27.4 us
    dot_general x24, matrix products, dot_halves(): jnp.dot(left[:, :half], low, preferred_element_type=f32)  24.7 us
    reduce_scatter x1, waiting for transfers between devices, local(): merged = lax.psum_scatter(merged, 'blk', scatter_dimension=0, tiled=True)  12.5 us
    all_gather x2, waiting for transfers between devices, local(): feat = lax.all_gather(hidden, 'mp', axis=1, tiled=True)  12.5 us
  transfers between devices with their start and end apart: 44, of which 20 were waited for; matrix products, arithmetic and copies ran while one was open for 23% of the time, Pallas kernels for 0%

profile of v2, /device:TPU:0, one launch (start us, length us, event | category | flops | bytes accessed | tf_op | source)
XLA Modules:
  0.0 381.2 jit_solution(7819934889911693366)
XLA Ops:
  6.5 4.1 %copy.76 = bf16[1,1024,1024]{1,2,0:T(8,128)(2,1)} copy(bf16[1,1024,1024]{2,1,0:T(8,128)(2,1)} %param.19) | data formatting | bytes 4194304 | tf_op args[8]
  10.6 3.1 constant_dynamic-slice_fusion.10
  13.7 2.3 copy.78
  17.2 2.7 pad_maximum_fusion
  22.6 6.2 %convolution_convert_fusion = bf16[128,4096]{1,0:T(8,128)(2,1)} fusion(bf16[320,4096]{1,0:T(8,128)(2,1)} %param.14, bf16[5120,320]{0,1:T(8,128)(2,1)S(1)} %copy-done, bf16[128,1280]{1,0:T(8,128)(2,1)} %get-tuple-element.110, bf16[128,1280]{1,0:T(8,128)(2,1)} %get-tuple-element.109, bf16[128,1280]{1,0:T(8,128)(2,1)} %get-tuple-element.108, ...), kind=kOutput, calls=%fused_computation | convolution fusion | flops 763404288 | bytes 8257536 | tf_op jit(solution)/shard_map/dot_general | solution.py:141
  29.0 2.5 dynamic-slice_bitcast_fusion
  33.7 2.3 broadcast_select_fusion
  37.3 2.9 collective-permute-start.1
  42.4 2.4 bitcast_select_fusion.2
  47.0 11.7 %reduce-scatter.5.cloned.1.call-done = bf16[128,1024]{1,0:T(8,128)(2,1)} async-done(((bf16[128,4096]{1,0:T(8,128)(2,1)}), bf16[128,1024]{1,0:T(8,128)(2,1)}) %reduce-scatter.5.cloned.1.call-update) | async-done | bytes 262160 | tf_op jit(solution)/shard_map/reduce_scatter | solution.py:142
  58.9 19.0 %collective-permute-done.2 = bf16[512,768]{1,0:T(8,128)(2,1)} collective-permute-done((bf16[512,768]{1,0:T(8,128)(2,1)}, bf16[512,768]{1,0:T(8,128)(2,1)}, u32[]{:S(2)}, u32[]{:S(2)}) %collective-permute-start.2) | collective-permute-done | bytes 786464 | tf_op jit(solution)/shard_map/ppermute | solution.py:17
  82.1 7.0 %collective-permute-done.10 = bf16[256,1024]{1,0:T(8,128)(2,1)} collective-permute-done((bf16[256,1024]{1,0:T(8,128)(2,1)S(1)}, bf16[256,1024]{1,0:T(8,128)(2,1)}, u32[]{:S(2)}, u32[]{:S(2)}) %collective-permute-start.10) | collective-permute-done | bytes 524320 | tf_op jit(solution)/shard_map/ppermute | solution.py:17
  89.1 2.2 collective-permute-start.9
  92.5 12.5 %reduce-scatter.7.cloned.1.call-done = bf16[32,1024]{1,0:T(8,128)(2,1)} async-done(((bf16[128,1024]{1,0:T(8,128)(2,1)}), bf16[32,1024]{1,0:T(8,128)(2,1)}) %reduce-scatter.7.cloned.1.call-update) | async-done | bytes 65552 | tf_op jit(solution)/shard_map/reduce_scatter | solution.py:145
  105.0 37.7 %all_gather.9 = bf16[256,1024]{1,0:T(8,128)(2,1)S(1)} all-gather(bf16[32,1024]{1,0:T(8,128)(2,1)} %reduce-scatter.7.cloned.1.call-done), channel_id=1, replica_groups=mesh['section'=2,'blk'=4,'mp'=4] {'section','blk'}, dimensions={0}, use_global_device_ids=true | all-gather | bytes 589824 | tf_op jit(solution)/shard_map/all_gather | solution.py:146
  146.0 13.2 %collective-permute-done.12 = bf16[256,1024]{1,0:T(8,128)(2,1)} collective-permute-done((bf16[256,1024]{1,0:T(8,128)(2,1)}, bf16[256,1024]{1,0:T(8,128)(2,1)}, u32[]{:S(2)}, u32[]{:S(2)}) %collective-permute-start.12) | collective-permute-done | bytes 524320 | tf_op jit(solution)/shard_map/ppermute | solution.py:17
  160.4 11.9 %all-gather.3.cloned.1.call-done = bf16[128,4096]{1,0:T(8,128)(2,1)} async-done(((bf16[128,1024]{1,0:T(8,128)(2,1)}), bf16[128,4096]{1,0:T(8,128)(2,1)}) %all-gather.3.cloned.1.call-update) | async-done | bytes 1048592 | tf_op jit(solution)/shard_map/all_gather | solution.py:179
  196.3 2.4 collective-permute-start.18
  211.5 9.8 %collective-permute-done.20 = bf16[512,768]{1,0:T(8,128)(2,1)} collective-permute-done((bf16[512,768]{1,0:T(8,128)(2,1)S(1)}, bf16[512,768]{1,0:T(8,128)(2,1)}, u32[]{:S(2)}, u32[]{:S(2)}) %collective-permute-start.20) | collective-permute-done | bytes 786464 | tf_op jit(solution)/shard_map/ppermute | solution.py:17
  241.3 2.2 collective-permute-start.24
  243.8 24.1 %reduce-scatter.9.cloned.1.call-done = bf16[128,1024]{1,0:T(8,128)(2,1)} async-done(((bf16[128,4096]{1,0:T(8,128)(2,1)}), bf16[128,1024]{1,0:T(8,128)(2,1)}) %reduce-scatter.9.cloned.1.call-update) | async-done | bytes 262160 | tf_op jit(solution)/shard_map/reduce_scatter | solution.py:236
  273.9 10.8 %collective-permute-done.26 = bf16[256,1024]{1,0:T(8,128)(2,1)S(1)} collective-permute-done((bf16[256,1024]{1,0:T(8,128)(2,1)S(1)}, bf16[256,1024]{1,0:T(8,128)(2,1)S(1)}, u32[]{:S(2)}, u32[]{:S(2)}) %collective-permute-start.26) | collective-permute-done | bytes 524320 | tf_op jit(solution)/shard_map/ppermute | solution.py:17
  286.3 9.5 %collective-permute-done.28 = bf16[256,1024]{1,0:T(8,128)(2,1)S(1)} collective-permute-done((bf16[256,1024]{1,0:T(8,128)(2,1)S(1)}, bf16[256,1024]{1,0:T(8,128)(2,1)S(1)}, u32[]{:S(2)}, u32[]{:S(2)}) %collective-permute-start.28) | collective-permute-done | bytes 524320 | tf_op jit(solution)/shard_map/ppermute | solution.py:17
  343.7 26.1 %reduce-scatter.11.cloned.1.call-done = bf16[128,1024]{1,0:T(8,128)(2,1)} async-done(((bf16[128,4096]{1,0:T(8,128)(2,1)}), bf16[128,1024]{1,0:T(8,128)(2,1)}) %reduce-scatter.11.cloned.1.call-update) | async-done | bytes 262160 | tf_op jit(solution)/shard_map/reduce_scatter | solution.py:236
  (304 shorter events, 138.0 us)
Async XLA Ops:
  6.5 52.1 %reduce-scatter.5.cloned.1.call-start = ((), (), s32[]{:S(2)}) async-start(), calls=%async_computation.4 | async-start | bytes 1310720 | tf_op jit(solution)/shard_map/reduce_scatter | solution.py:142
  28.9 76.1 %reduce-scatter.7.cloned.1.call-start = ((), (), s32[]{:S(2)}) async-start(), calls=%async_computation.5 | async-start | bytes 327680 | tf_op jit(solution)/shard_map/reduce_scatter | solution.py:145
  37.3 21.6 %collective-permute-start.1 = (bf16[512,768]{1,0:T(8,128)(2,1)}, bf16[512,768]{1,0:T(8,128)(2,1)}, u32[]{:S(2)}, u32[]{:S(2)}) collective-permute-start(bf16[512,768]{1,0:T(8,128)(2,1)} %get-tuple-element.48), channel_id=1, source_target_pairs={{0,4},{4,0},{8,12},{12,8},{1,5},{5,1},{9,13},{13,9},{2,6},{6,2},{1... | collective-permute-start | bytes 2359304 | tf_op jit(solution)/shard_map/ppermute | solution.py:17
  40.3 37.6 %collective-permute-start.3 = (bf16[512,768]{1,0:T(8,128)(2,1)}, bf16[512,768]{1,0:T(8,128)(2,1)}, u32[]{:S(2)}, u32[]{:S(2)}) collective-permute-start(bf16[512,768]{1,0:T(8,128)(2,1)} %get-tuple-element.48), channel_id=1, source_target_pairs={{0,8},{4,12},{8,0},{12,4},{1,9},{5,13},{9,1},{13,5},{2,10},{6,14},... | collective-permute-start | bytes 2359304 | tf_op jit(solution)/shard_map/ppermute | solution.py:17
  41.8 36.1 %collective-permute-start.2 = (bf16[512,768]{1,0:T(8,128)(2,1)}, bf16[512,768]{1,0:T(8,128)(2,1)}, u32[]{:S(2)}, u32[]{:S(2)}) collective-permute-start(bf16[512,768]{1,0:T(8,128)(2,1)} %get-tuple-element.49), channel_id=1, source_target_pairs={{0,8},{4,12},{8,0},{12,4},{1,9},{5,13},{9,1},{13,5},{2,10},{6,14},... | collective-permute-start | bytes 2359304 | tf_op jit(solution)/shard_map/ppermute | solution.py:17
  42.3 35.6 %collective-permute-start.4 = (bf16[512,768]{1,0:T(8,128)(2,1)}, bf16[512,768]{1,0:T(8,128)(2,1)}, u32[]{:S(2)}, u32[]{:S(2)}) collective-permute-start(bf16[512,768]{1,0:T(8,128)(2,1)} %get-tuple-element.49), channel_id=1, source_target_pairs={{0,4},{4,0},{8,12},{12,8},{1,5},{5,1},{9,13},{13,9},{2,6},{6,2},{1... | collective-permute-start | bytes 2359304 | tf_op jit(solution)/shard_map/ppermute | solution.py:17
  44.9 44.3 %collective-permute-start.10 = (bf16[256,1024]{1,0:T(8,128)(2,1)S(1)}, bf16[256,1024]{1,0:T(8,128)(2,1)}, u32[]{:S(2)}, u32[]{:S(2)}) collective-permute-start(bf16[256,1024]{1,0:T(8,128)(2,1)S(1)} %get-tuple-element.55), channel_id=1, source_target_pairs={{0,8},{4,12},{8,0},{12,4},{1,9},{5,13},{9,1},{13,5},{2,10},{6,14},... | collective-permute-start | bytes 1572872 | tf_op jit(solution)/shard_map/ppermute | solution.py:17
  77.9 64.9 %collective-permute-start.5 = (bf16[512,768]{1,0:T(8,128)(2,1)}, bf16[512,768]{1,0:T(8,128)(2,1)}, u32[]{:S(2)}, u32[]{:S(2)}) collective-permute-start(bf16[512,768]{1,0:T(8,128)(2,1)} %collective-permute-done.1), channel_id=1, source_target_pairs={{0,8},{4,12},{8,0},{12,4},{1,9},{5,13},{9,1},{13,5},{2,10},{6,14},... | collective-permute-start | bytes 2359304 | tf_op jit(solution)/shard_map/ppermute | solution.py:17
  79.4 63.4 %collective-permute-start.6 = (bf16[512,768]{1,0:T(8,128)(2,1)}, bf16[512,768]{1,0:T(8,128)(2,1)}, u32[]{:S(2)}, u32[]{:S(2)}) collective-permute-start(bf16[512,768]{1,0:T(8,128)(2,1)} %collective-permute-done.2), channel_id=1, source_target_pairs={{0,4},{4,0},{8,12},{12,8},{1,5},{5,1},{9,13},{13,9},{2,6},{6,2},{1... | collective-permute-start | bytes 2359304 | tf_op jit(solution)/shard_map/ppermute | solution.py:17
  80.0 92.3 %all-gather.3.cloned.1.call-start = ((), (), s32[]{:S(2)}) async-start(), calls=%async_computation.6 | async-start | bytes 1310720 | tf_op jit(solution)/shard_map/all_gather | solution.py:179
  80.1 62.8 %collective-permute-start.8 = (bf16[256,1024]{1,0:T(8,128)(2,1)S(1)}, bf16[256,1024]{1,0:T(8,128)(2,1)}, u32[]{:S(2)}, u32[]{:S(2)}) collective-permute-start(bf16[256,1024]{1,0:T(8,128)(2,1)S(1)} %get-tuple-element.55), channel_id=1, source_target_pairs={{0,4},{4,0},{8,12},{12,8},{1,5},{5,1},{9,13},{13,9},{2,6},{6,2},{1... | collective-permute-start | bytes 1572872 | tf_op jit(solution)/shard_map/ppermute | solution.py:17
  81.6 61.2 %collective-permute-start.11 = (bf16[256,1024]{1,0:T(8,128)(2,1)S(1)}, bf16[256,1024]{1,0:T(8,128)(2,1)}, u32[]{:S(2)}, u32[]{:S(2)}) collective-permute-start(bf16[256,1024]{1,0:T(8,128)(2,1)S(1)} %get-tuple-element.56), channel_id=1, source_target_pairs={{0,4},{4,0},{8,12},{12,8},{1,5},{5,1},{9,13},{13,9},{2,6},{6,2},{1... | collective-permute-start | bytes 1572872 | tf_op jit(solution)/shard_map/ppermute | solution.py:17
  89.1 53.7 %collective-permute-start.9 = (bf16[256,1024]{1,0:T(8,128)(2,1)S(1)}, bf16[256,1024]{1,0:T(8,128)(2,1)}, u32[]{:S(2)}, u32[]{:S(2)}) collective-permute-start(bf16[256,1024]{1,0:T(8,128)(2,1)S(1)} %get-tuple-element.56), channel_id=1, source_target_pairs={{0,8},{4,12},{8,0},{12,4},{1,9},{5,13},{9,1},{13,5},{2,10},{6,14},... | collective-permute-start | bytes 1572872 | tf_op jit(solution)/shard_map/ppermute | solution.py:17
  143.9 124.0 %reduce-scatter.9.cloned.1.call-start = ((), (), s32[]{:S(2)}) async-start(), calls=%async_computation.7 | async-start | bytes 1310720 | tf_op jit(solution)/shard_map/reduce_scatter | solution.py:236
  177.4 34.1 %collective-permute-start.19 = (bf16[512,768]{1,0:T(8,128)(2,1)}, bf16[512,768]{1,0:T(8,128)(2,1)}, u32[]{:S(2)}, u32[]{:S(2)}) collective-permute-start(bf16[512,768]{1,0:T(8,128)(2,1)} %get-tuple-element.65), channel_id=1, source_target_pairs={{0,4},{4,0},{8,12},{12,8},{1,5},{5,1},{9,13},{13,9},{2,6},{6,2},{1... | collective-permute-start | bytes 2359304 | tf_op jit(solution)/shard_map/ppermute | solution.py:17
  178.9 42.4 %collective-permute-start.21 = (bf16[512,768]{1,0:T(8,128)(2,1)}, bf16[512,768]{1,0:T(8,128)(2,1)}, u32[]{:S(2)}, u32[]{:S(2)}) collective-permute-start(bf16[512,768]{1,0:T(8,128)(2,1)} %get-tuple-element.65), channel_id=1, source_target_pairs={{0,8},{4,12},{8,0},{12,4},{1,9},{5,13},{9,1},{13,5},{2,10},{6,14},... | collective-permute-start | bytes 2359304 | tf_op jit(solution)/shard_map/ppermute | solution.py:17
  241.3 55.1 %all-gather.5.cloned.1.call-start = ((), (), s32[]{:S(2)}) async-start(), calls=%async_computation.8 | async-start | bytes 1310720 | tf_op jit(solution)/shard_map/all_gather | solution.py:179
  241.3 28.3 %collective-permute-start.24 = (bf16[512,768]{1,0:T(8,128)(2,1)}, bf16[512,768]{1,0:T(8,128)(2,1)}, u32[]{:S(2)}, u32[]{:S(2)}) collective-permute-start(bf16[512,768]{1,0:T(8,128)(2,1)} %collective-permute-done.19), channel_id=1, source_target_pairs={{0,8},{4,12},{8,0},{12,4},{1,9},{5,13},{9,1},{13,5},{2,10},{6,14},... | collective-permute-start | bytes 2359304 | tf_op jit(solution)/shard_map/ppermute | solution.py:17
  243.5 26.1 %collective-permute-start.25 = (bf16[512,768]{1,0:T(8,128)(2,1)}, bf16[512,768]{1,0:T(8,128)(2,1)}, u32[]{:S(2)}, u32[]{:S(2)}) collective-permute-start(bf16[512,768]{1,0:T(8,128)(2,1)} %collective-permute-done.20), channel_id=1, source_target_pairs={{0,4},{4,0},{8,12},{12,8},{1,5},{5,1},{9,13},{13,9},{2,6},{6,2},{1... | collective-permute-start | bytes 2359304 | tf_op jit(solution)/shard_map/ppermute | solution.py:17
  269.7 100.1 %reduce-scatter.11.cloned.1.call-start = ((), (), s32[]{:S(2)}) async-start(), calls=%async_computation.9 | async-start | bytes 1310720 | tf_op jit(solution)/shard_map/reduce_scatter | solution.py:236
  272.8 23.0 %collective-permute-start.28 = (bf16[256,1024]{1,0:T(8,128)(2,1)S(1)}, bf16[256,1024]{1,0:T(8,128)(2,1)S(1)}, u32[]{:S(2)}, u32[]{:S(2)}) collective-permute-start(bf16[256,1024]{1,0:T(8,128)(2,1)S(1)} %get-tuple-element.71), channel_id=1, source_target_pairs={{0,8},{4,12},{8,0},{12,4},{1,9},{5,13},{9,1},{13,5},{2,10},{6,14},... | collective-permute-start | bytes 1572872 | tf_op jit(solution)/shard_map/ppermute | solution.py:17
  273.4 22.4 %collective-permute-start.29 = (bf16[256,1024]{1,0:T(8,128)(2,1)S(1)}, bf16[256,1024]{1,0:T(8,128)(2,1)}, u32[]{:S(2)}, u32[]{:S(2)}) collective-permute-start(bf16[256,1024]{1,0:T(8,128)(2,1)S(1)} %get-tuple-element.72), channel_id=1, source_target_pairs={{0,4},{4,0},{8,12},{12,8},{1,5},{5,1},{9,13},{13,9},{2,6},{6,2},{1... | collective-permute-start | bytes 1572872 | tf_op jit(solution)/shard_map/ppermute | solution.py:17
  299.6 36.1 %collective-permute-start.35 = (bf16[256,1024]{1,0:T(8,128)(2,1)}, bf16[256,1024]{1,0:T(8,128)(2,1)}, u32[]{:S(2)}, u32[]{:S(2)}) collective-permute-start(bf16[256,1024]{1,0:T(8,128)(2,1)} %collective-permute-done.27), channel_id=1, source_target_pairs={{0,4},{4,0},{8,12},{12,8},{1,5},{5,1},{9,13},{13,9},{2,6},{6,2},{1... | collective-permute-start | bytes 1572872 | tf_op jit(solution)/shard_map/ppermute | solution.py:17
  301.1 36.4 %collective-permute-start.34 = (bf16[256,1024]{1,0:T(8,128)(2,1)}, bf16[256,1024]{1,0:T(8,128)(2,1)}, u32[]{:S(2)}, u32[]{:S(2)}) collective-permute-start(bf16[256,1024]{1,0:T(8,128)(2,1)} %copy-done.12), channel_id=1, source_target_pairs={{0,8},{4,12},{8,0},{12,4},{1,9},{5,13},{9,1},{13,5},{2,10},{6,14},... | collective-permute-start | bytes 1572872 | tf_op jit(solution)/shard_map/ppermute | solution.py:17
  (47 other events, 948.8 us)
Sparse Core Ops, SparseCore 0:
  29.0 29.5 reduce-scatter.4
  80.1 24.8 reduce-scatter.6
  144.0 28.2 all-gather.2
  241.4 26.4 reduce-scatter.8
  269.8 26.5 all-gather.4
  343.9 25.8 reduce-scatter.10

commit v3 on v2

--- a/solution.py
+++ b/solution.py
@@ -143,7 +143,20 @@
     merged, in_near = together(merged, in_near)
     in_far = far_blk(in_near)
     merged = lax.psum_scatter(merged, "blk", scatter_dimension=0, tiled=True)
-    visual = lax.all_gather(merged, ("section", "blk"), axis=0, tiled=True)
+    visual_at = positions
+    if nb == 4:
+        visual = jnp.concatenate([merged] + [swap_blk(merged, k) for k in (1, 2, 3)], axis=0)
+        visual = jnp.concatenate([visual, other_section(visual)], axis=0)
+        parts = positions.reshape(2 * nb, -1)
+        visual_at = jnp.concatenate(
+            [
+                lax.dynamic_index_in_dim(parts, h * nb + (cycle ^ k), 0, keepdims=False)
+                for h in (section, 1 - section)
+                for k in range(nb)
+            ]
+        )
+    else:
+        visual = lax.all_gather(merged, ("section", "blk"), axis=0, tiled=True)
     visual, in_far, o_near = together(visual, in_far, o_near)
 
     def at(half, cyc):
@@ -166,7 +179,7 @@
     cosine, sine = rope_tables(row_where, head_size)
 
     mine_where = at(section, cycle)
-    is_visual = positions[None, :] == mine_where[:, None]
+    is_visual = visual_at[None, :] == mine_where[:, None]
     picked = jnp.dot(is_visual.astype(bf16), visual, preferred_element_type=f32).astype(bf16)
     text = lax.dynamic_slice_in_dim(text_embeds, section * half_rows, half_rows, 1)
     hidden = jnp.where(

time: 384 us -> 393 us (1.023)
  blocking collectives: 37.7 us -> 0 us
  waiting for transfers between devices: 164 us -> 200 us
  local copies, waits for them, and re-layouts: 32.1 us -> 45.4 us
  matrix products: 63.8 us -> 54.1 us
  other arithmetic: 31.7 us -> 36.1 us
    all_gather x1 -> x0, blocking collectives: 37.7 us -> none  [local(): visual = lax.all_gather(merged, ('section', 'blk'), axis=0, tiled=True)]
    ppermute x30 -> x33, waiting for transfers between devices: 75.5 us -> 108 us  [swap_blk(): lax.ppermute(value, 'blk', [(i, i ^ bit) for i in range(lax.axis_size('bl...]
    unnamed x74 -> x118, local copies, waits for them, and re-layouts: 6.19 us -> 19.7 us
    reduce_scatter x1, waiting for transfers between devices: 12.5 us -> 21.7 us  [local(): merged = lax.psum_scatter(merged, 'blk', scatter_dimension=0, tiled=True)]
    all_gather x2, waiting for transfers between devices: 12.5 us -> 4.32 us  [local(): feat = lax.all_gather(hidden, 'mp', axis=1, tiled=True)]
    dot_general x24, matrix products: 27.4 us -> 21.3 us  [dot_halves(): jnp.dot(left[:, half:], high, preferred_element_type=f32)]
    dot_general x24, matrix products: 24.7 us -> 20.4 us  [dot_halves(): jnp.dot(left[:, :half], low, preferred_element_type=f32)]
    ppermute x30 -> x33, starting transfers between devices: 35.6 us -> 38.6 us  [swap_blk(): lax.ppermute(value, 'blk', [(i, i ^ bit) for i in range(lax.axis_size('bl...]
  transfers between devices with their start and end apart: 44 -> 48, of which waited for: 20 -> 23; matrix products, arithmetic and copies ran while one was open for 23% -> 25% of each run, Pallas kernels for 0% -> 0%
where the time goes in v3:
time: 393 us; the launch traced here: 391 us
  waiting for transfers between devices  200 us (51%)
  matrix products  54.1 us (14%)
  local copies, waits for them, and re-layouts  45.4 us (12%)
  starting transfers between devices  40 us (10%)
  other arithmetic  36.1 us (9%)
  between operations  15 us (4%)
    ppermute x33, waiting for transfers between devices, swap_blk(): lax.ppermute(value, 'blk', [(i, i ^ bit) for i in range(lax.axis_size('bl...  108 us
    reduce_scatter x2, waiting for transfers between devices, local(): term = lax.psum_scatter(term, 'mp', scatter_dimension=1, tiled=True)  50.2 us
    ppermute x33, starting transfers between devices, swap_blk(): lax.ppermute(value, 'blk', [(i, i ^ bit) for i in range(lax.axis_size('bl...  38.6 us
    reduce_scatter x1, waiting for transfers between devices, local(): merged = lax.psum_scatter(merged, 'blk', scatter_dimension=0, tiled=True)  21.7 us
    dot_general x24, matrix products, dot_halves(): jnp.dot(left[:, half:], high, preferred_element_type=f32)  21.3 us
    dot_general x24, matrix products, dot_halves(): jnp.dot(left[:, :half], low, preferred_element_type=f32)  20.4 us
    unnamed x118, local copies, waits for them, and re-layouts  19.7 us
    reduce_scatter x1, waiting for transfers between devices, local(): lax.psum_scatter(partial_merge, 'mp', scatter_dimension=1, tiled=True)  15 us
  transfers between devices with their start and end apart: 48, of which 23 were waited for; matrix products, arithmetic and copies ran while one was open for 25% of the time, Pallas kernels for 0%

profile of v3, /device:TPU:0, one launch (start us, length us, event | category | flops | bytes accessed | tf_op | source)
XLA Modules:
  0.0 391.0 jit_solution(15851068205000397778)
XLA Ops:
  6.5 4.1 %copy.76 = bf16[1,1024,1024]{1,2,0:T(8,128)(2,1)} copy(bf16[1,1024,1024]{2,1,0:T(8,128)(2,1)} %param.19) | data formatting | bytes 4194304 | tf_op args[8]
  10.6 3.0 constant_dynamic-slice_fusion.10
  13.6 2.3 copy.78
  17.1 2.8 pad_maximum_fusion
  22.7 6.2 %convolution_convert_fusion = bf16[128,4096]{1,0:T(8,128)(2,1)} fusion(bf16[320,4096]{1,0:T(8,128)(2,1)} %param.14, bf16[5120,320]{0,1:T(8,128)(2,1)S(1)} %copy-done, bf16[128,1280]{1,0:T(8,128)(2,1)} %get-tuple-element.110, bf16[128,1280]{1,0:T(8,128)(2,1)} %get-tuple-element.109, bf16[128,1280]{1,0:T(8,128)(2,1)} %get-tuple-element.108, ...), kind=kOutput, calls=%fused_computation | convolution fusion | flops 763404288 | bytes 8257536 | tf_op jit(solution)/shard_map/dot_general | solution.py:141
  29.0 2.4 dynamic-slice_bitcast_fusion
  34.7 2.3 broadcast_select_fusion
  37.1 3.0 collective-permute-start.1
  43.6 15.0 %reduce-scatter.5.cloned.1.call-done = bf16[128,1024]{1,0:T(8,128)(2,1)} async-done(((bf16[128,4096]{1,0:T(8,128)(2,1)}), bf16[128,1024]{1,0:T(8,128)(2,1)}) %reduce-scatter.5.cloned.1.call-update) | async-done | bytes 262160 | tf_op jit(solution)/shard_map/reduce_scatter | solution.py:142
  58.6 17.7 %collective-permute-done.2 = bf16[512,768]{1,0:T(8,128)(2,1)} collective-permute-done((bf16[512,768]{1,0:T(8,128)(2,1)S(1)}, bf16[512,768]{1,0:T(8,128)(2,1)}, u32[]{:S(2)}, u32[]{:S(2)}) %collective-permute-start.2) | collective-permute-done | bytes 786464 | tf_op jit(solution)/shard_map/ppermute | solution.py:17
  76.4 2.6 bitcast_select_fusion.2
  79.6 21.7 %reduce-scatter.7.cloned.1.call-done = bf16[32,1024]{1,0:T(8,128)(2,1)} async-done(((bf16[128,1024]{1,0:T(8,128)(2,1)}), bf16[32,1024]{1,0:T(8,128)(2,1)}) %reduce-scatter.7.cloned.1.call-update) | async-done | bytes 65552 | tf_op jit(solution)/shard_map/reduce_scatter | solution.py:145
  121.2 34.2 %collective-permute-done.13 = bf16[256,1024]{1,0:T(8,128)(2,1)S(1)} collective-permute-done((bf16[256,1024]{1,0:T(8,128)(2,1)S(1)}, bf16[256,1024]{1,0:T(8,128)(2,1)S(1)}, u32[]{:S(2)}, u32[]{:S(2)}) %collective-permute-start.13) | collective-permute-done | bytes 524320 | tf_op jit(solution)/shard_map/ppermute | solution.py:17
  172.2 11.9 %collective-permute-done.16 = bf16[256,1024]{1,0:T(8,128)(2,1)} collective-permute-done((bf16[256,1024]{1,0:T(8,128)(2,1)}, bf16[256,1024]{1,0:T(8,128)(2,1)}, u32[]{:S(2)}, u32[]{:S(2)}) %collective-permute-start.16) | collective-permute-done | bytes 524320 | tf_op jit(solution)/shard_map/ppermute | solution.py:17
  184.4 3.7 all-gather.3.cloned.1.call-done
  208.0 2.4 collective-permute-start.22
  212.5 4.3 %collective-permute-done.20 = bf16[256,256]{1,0:T(8,128)(2,1)} collective-permute-done((bf16[256,256]{1,0:T(8,128)(2,1)}, bf16[256,256]{1,0:T(8,128)(2,1)}, u32[]{:S(2)}, u32[]{:S(2)}) %collective-permute-start.20) | collective-permute-done | bytes 131104 | tf_op jit(solution)/shard_map/ppermute | solution.py:17
  227.4 9.8 %collective-permute-done.24 = bf16[512,768]{1,0:T(8,128)(2,1)} collective-permute-done((bf16[512,768]{1,0:T(8,128)(2,1)S(1)}, bf16[512,768]{1,0:T(8,128)(2,1)}, u32[]{:S(2)}, u32[]{:S(2)}) %collective-permute-start.24) | collective-permute-done | bytes 786464 | tf_op jit(solution)/shard_map/ppermute | solution.py:17
  250.5 2.8 collective-permute-start.28
  253.6 24.1 %reduce-scatter.9.cloned.1.call-done = bf16[128,1024]{1,0:T(8,128)(2,1)} async-done(((bf16[128,4096]{1,0:T(8,128)(2,1)}), bf16[128,1024]{1,0:T(8,128)(2,1)}) %reduce-scatter.9.cloned.1.call-update) | async-done | bytes 262160 | tf_op jit(solution)/shard_map/reduce_scatter | solution.py:249
  283.7 10.8 %collective-permute-done.30 = bf16[256,1024]{1,0:T(8,128)(2,1)S(1)} collective-permute-done((bf16[256,1024]{1,0:T(8,128)(2,1)S(1)}, bf16[256,1024]{1,0:T(8,128)(2,1)S(1)}, u32[]{:S(2)}, u32[]{:S(2)}) %collective-permute-start.30) | collective-permute-done | bytes 524320 | tf_op jit(solution)/shard_map/ppermute | solution.py:17
  296.1 9.5 %collective-permute-done.32 = bf16[256,1024]{1,0:T(8,128)(2,1)S(1)} collective-permute-done((bf16[256,1024]{1,0:T(8,128)(2,1)S(1)}, bf16[256,1024]{1,0:T(8,128)(2,1)S(1)}, u32[]{:S(2)}, u32[]{:S(2)}) %collective-permute-start.32) | collective-permute-done | bytes 524320 | tf_op jit(solution)/shard_map/ppermute | solution.py:17
  324.8 2.1 collective-permute-start.37
  353.5 26.1 %reduce-scatter.11.cloned.1.call-done = bf16[128,1024]{1,0:T(8,128)(2,1)} async-done(((bf16[128,4096]{1,0:T(8,128)(2,1)}), bf16[128,1024]{1,0:T(8,128)(2,1)}) %reduce-scatter.11.cloned.1.call-update) | async-done | bytes 262160 | tf_op jit(solution)/shard_map/reduce_scatter | solution.py:249
  (360 shorter events, 151.3 us)
Async XLA Ops:
  6.5 52.1 %reduce-scatter.5.cloned.1.call-start = ((), (), s32[]{:S(2)}) async-start(), calls=%async_computation.4 | async-start | bytes 1310720 | tf_op jit(solution)/shard_map/reduce_scatter | solution.py:142
  28.9 72.4 %reduce-scatter.7.cloned.1.call-start = ((), (), s32[]{:S(2)}) async-start(), calls=%async_computation.5 | async-start | bytes 327680 | tf_op jit(solution)/shard_map/reduce_scatter | solution.py:145
  31.3 45.1 %collective-permute-start.11 = (bf16[512,1024]{1,0:T(8,128)(2,1)}, bf16[512,1024]{1,0:T(8,128)(2,1)}, u32[]{:S(2)}, u32[]{:S(2)}) collective-permute-start(bf16[512,1024]{1,0:T(8,128)(2,1)} %dynamic-slice_bitcast_fusion), channel_id=1, source_target_pairs={{0,16},{16,0},{1,17},{17,1},{2,18},{18,2},{3,19},{19,3},{4,20},{20... | collective-permute-start | bytes 3145736 | tf_op jit(solution)/shard_map/ppermute | solution.py:13
  40.1 36.2 %collective-permute-start.3 = (bf16[512,768]{1,0:T(8,128)(2,1)S(1)}, bf16[512,768]{1,0:T(8,128)(2,1)}, u32[]{:S(2)}, u32[]{:S(2)}) collective-permute-start(bf16[512,768]{1,0:T(8,128)(2,1)S(1)} %get-tuple-element.48), channel_id=1, source_target_pairs={{0,8},{4,12},{8,0},{12,4},{1,9},{5,13},{9,1},{13,5},{2,10},{6,14},... | collective-permute-start | bytes 2359304 | tf_op jit(solution)/shard_map/ppermute | solution.py:17
  41.6 34.7 %collective-permute-start.2 = (bf16[512,768]{1,0:T(8,128)(2,1)S(1)}, bf16[512,768]{1,0:T(8,128)(2,1)}, u32[]{:S(2)}, u32[]{:S(2)}) collective-permute-start(bf16[512,768]{1,0:T(8,128)(2,1)S(1)} %get-tuple-element.49), channel_id=1, source_target_pairs={{0,8},{4,12},{8,0},{12,4},{1,9},{5,13},{9,1},{13,5},{2,10},{6,14},... | collective-permute-start | bytes 2359304 | tf_op jit(solution)/shard_map/ppermute | solution.py:17
  42.1 34.2 %collective-permute-start.4 = (bf16[512,768]{1,0:T(8,128)(2,1)S(1)}, bf16[512,768]{1,0:T(8,128)(2,1)}, u32[]{:S(2)}, u32[]{:S(2)}) collective-permute-start(bf16[512,768]{1,0:T(8,128)(2,1)S(1)} %get-tuple-element.49), channel_id=1, source_target_pairs={{0,4},{4,0},{8,12},{12,8},{1,5},{5,1},{9,13},{13,9},{2,6},{6,2},{1... | collective-permute-start | bytes 2359304 | tf_op jit(solution)/shard_map/ppermute | solution.py:17
  76.3 111.8 %all-gather.3.cloned.1.call-start = ((), (), s32[]{:S(2)}) async-start(), calls=%async_computation.6 | async-start | bytes 1310720 | tf_op jit(solution)/shard_map/all_gather | solution.py:192
  79.2 38.3 %collective-permute-start.12 = (bf16[256,1024]{1,0:T(8,128)(2,1)S(1)}, bf16[256,1024]{1,0:T(8,128)(2,1)}, u32[]{:S(2)}, u32[]{:S(2)}) collective-permute-start(bf16[256,1024]{1,0:T(8,128)(2,1)S(1)} %get-tuple-element.55), channel_id=1, source_target_pairs={{0,4},{4,0},{8,12},{12,8},{1,5},{5,1},{9,13},{13,9},{2,6},{6,2},{1... | collective-permute-start | bytes 1572872 | tf_op jit(solution)/shard_map/ppermute | solution.py:17
  111.7 44.7 %collective-permute-start.10 = (bf16[512,768]{1,0:T(8,128)(2,1)}, bf16[512,768]{1,0:T(8,128)(2,1)S(1)}, u32[]{:S(2)}, u32[]{:S(2)}) collective-permute-start(bf16[512,768]{1,0:T(8,128)(2,1)} %collective-permute-done.2), channel_id=1, source_target_pairs={{0,4},{4,0},{8,12},{12,8},{1,5},{5,1},{9,13},{13,9},{2,6},{6,2},{1... | collective-permute-start | bytes 2359304 | tf_op jit(solution)/shard_map/ppermute | solution.py:17
  113.1 43.3 %collective-permute-start.9 = (bf16[512,768]{1,0:T(8,128)(2,1)}, bf16[512,768]{1,0:T(8,128)(2,1)S(1)}, u32[]{:S(2)}, u32[]{:S(2)}) collective-permute-start(bf16[512,768]{1,0:T(8,128)(2,1)} %collective-permute-done.1), channel_id=1, source_target_pairs={{0,8},{4,12},{8,0},{12,4},{1,9},{5,13},{9,1},{13,5},{2,10},{6,14},... | collective-permute-start | bytes 2359304 | tf_op jit(solution)/shard_map/ppermute | solution.py:17
  115.9 39.5 %collective-permute-start.14 = (bf16[256,1024]{1,0:T(8,128)(2,1)S(1)}, bf16[256,1024]{1,0:T(8,128)(2,1)S(1)}, u32[]{:S(2)}, u32[]{:S(2)}) collective-permute-start(bf16[256,1024]{1,0:T(8,128)(2,1)S(1)} %get-tuple-element.55), channel_id=1, source_target_pairs={{0,8},{4,12},{8,0},{12,4},{1,9},{5,13},{9,1},{13,5},{2,10},{6,14},... | collective-permute-start | bytes 1572872 | tf_op jit(solution)/shard_map/ppermute | solution.py:17
  117.5 38.0 %collective-permute-start.13 = (bf16[256,1024]{1,0:T(8,128)(2,1)S(1)}, bf16[256,1024]{1,0:T(8,128)(2,1)S(1)}, u32[]{:S(2)}, u32[]{:S(2)}) collective-permute-start(bf16[256,1024]{1,0:T(8,128)(2,1)S(1)} %get-tuple-element.56), channel_id=1, source_target_pairs={{0,8},{4,12},{8,0},{12,4},{1,9},{5,13},{9,1},{13,5},{2,10},{6,14},... | collective-permute-start | bytes 1572872 | tf_op jit(solution)/shard_map/ppermute | solution.py:17
  118.0 37.4 %collective-permute-start.15 = (bf16[256,1024]{1,0:T(8,128)(2,1)S(1)}, bf16[256,1024]{1,0:T(8,128)(2,1)S(1)}, u32[]{:S(2)}, u32[]{:S(2)}) collective-permute-start(bf16[256,1024]{1,0:T(8,128)(2,1)S(1)} %get-tuple-element.56), channel_id=1, source_target_pairs={{0,4},{4,0},{8,12},{12,8},{1,5},{5,1},{9,13},{13,9},{2,6},{6,2},{1... | collective-permute-start | bytes 1572872 | tf_op jit(solution)/shard_map/ppermute | solution.py:17
  160.0 117.7 %reduce-scatter.9.cloned.1.call-start = ((), (), s32[]{:S(2)}) async-start(), calls=%async_computation.7 | async-start | bytes 1310720 | tf_op jit(solution)/shard_map/reduce_scatter | solution.py:249
  193.4 34.1 %collective-permute-start.23 = (bf16[512,768]{1,0:T(8,128)(2,1)}, bf16[512,768]{1,0:T(8,128)(2,1)}, u32[]{:S(2)}, u32[]{:S(2)}) collective-permute-start(bf16[512,768]{1,0:T(8,128)(2,1)} %get-tuple-element.65), channel_id=1, source_target_pairs={{0,4},{4,0},{8,12},{12,8},{1,5},{5,1},{9,13},{13,9},{2,6},{6,2},{1... | collective-permute-start | bytes 2359304 | tf_op jit(solution)/shard_map/ppermute | solution.py:17
  194.8 42.4 %collective-permute-start.25 = (bf16[512,768]{1,0:T(8,128)(2,1)}, bf16[512,768]{1,0:T(8,128)(2,1)}, u32[]{:S(2)}, u32[]{:S(2)}) collective-permute-start(bf16[512,768]{1,0:T(8,128)(2,1)} %get-tuple-element.65), channel_id=1, source_target_pairs={{0,8},{4,12},{8,0},{12,4},{1,9},{5,13},{9,1},{13,5},{2,10},{6,14},... | collective-permute-start | bytes 2359304 | tf_op jit(solution)/shard_map/ppermute | solution.py:17
  250.4 55.8 %all-gather.5.cloned.1.call-start = ((), (), s32[]{:S(2)}) async-start(), calls=%async_computation.8 | async-start | bytes 1310720 | tf_op jit(solution)/shard_map/all_gather | solution.py:192
  250.5 29.0 %collective-permute-start.28 = (bf16[512,768]{1,0:T(8,128)(2,1)}, bf16[512,768]{1,0:T(8,128)(2,1)}, u32[]{:S(2)}, u32[]{:S(2)}) collective-permute-start(bf16[512,768]{1,0:T(8,128)(2,1)} %collective-permute-done.23), channel_id=1, source_target_pairs={{0,8},{4,12},{8,0},{12,4},{1,9},{5,13},{9,1},{13,5},{2,10},{6,14},... | collective-permute-start | bytes 2359304 | tf_op jit(solution)/shard_map/ppermute | solution.py:17
  253.3 26.2 %collective-permute-start.29 = (bf16[512,768]{1,0:T(8,128)(2,1)}, bf16[512,768]{1,0:T(8,128)(2,1)}, u32[]{:S(2)}, u32[]{:S(2)}) collective-permute-start(bf16[512,768]{1,0:T(8,128)(2,1)} %collective-permute-done.24), channel_id=1, source_target_pairs={{0,4},{4,0},{8,12},{12,8},{1,5},{5,1},{9,13},{13,9},{2,6},{6,2},{1... | collective-permute-start | bytes 2359304 | tf_op jit(solution)/shard_map/ppermute | solution.py:17
  279.5 100.1 %reduce-scatter.11.cloned.1.call-start = ((), (), s32[]{:S(2)}) async-start(), calls=%async_computation.9 | async-start | bytes 1310720 | tf_op jit(solution)/shard_map/reduce_scatter | solution.py:249
  282.6 23.0 %collective-permute-start.32 = (bf16[256,1024]{1,0:T(8,128)(2,1)S(1)}, bf16[256,1024]{1,0:T(8,128)(2,1)S(1)}, u32[]{:S(2)}, u32[]{:S(2)}) collective-permute-start(bf16[256,1024]{1,0:T(8,128)(2,1)S(1)} %get-tuple-element.71), channel_id=1, source_target_pairs={{0,8},{4,12},{8,0},{12,4},{1,9},{5,13},{9,1},{13,5},{2,10},{6,14},... | collective-permute-start | bytes 1572872 | tf_op jit(solution)/shard_map/ppermute | solution.py:17
  283.2 22.4 %collective-permute-start.33 = (bf16[256,1024]{1,0:T(8,128)(2,1)S(1)}, bf16[256,1024]{1,0:T(8,128)(2,1)}, u32[]{:S(2)}, u32[]{:S(2)}) collective-permute-start(bf16[256,1024]{1,0:T(8,128)(2,1)S(1)} %get-tuple-element.72), channel_id=1, source_target_pairs={{0,4},{4,0},{8,12},{12,8},{1,5},{5,1},{9,13},{13,9},{2,6},{6,2},{1... | collective-permute-start | bytes 1572872 | tf_op jit(solution)/shard_map/ppermute | solution.py:17
  309.4 36.1 %collective-permute-start.39 = (bf16[256,1024]{1,0:T(8,128)(2,1)}, bf16[256,1024]{1,0:T(8,128)(2,1)}, u32[]{:S(2)}, u32[]{:S(2)}) collective-permute-start(bf16[256,1024]{1,0:T(8,128)(2,1)} %collective-permute-done.31), channel_id=1, source_target_pairs={{0,4},{4,0},{8,12},{12,8},{1,5},{5,1},{9,13},{13,9},{2,6},{6,2},{1... | collective-permute-start | bytes 1572872 | tf_op jit(solution)/shard_map/ppermute | solution.py:17
  310.9 36.4 %collective-permute-start.38 = (bf16[256,1024]{1,0:T(8,128)(2,1)}, bf16[256,1024]{1,0:T(8,128)(2,1)}, u32[]{:S(2)}, u32[]{:S(2)}) collective-permute-start(bf16[256,1024]{1,0:T(8,128)(2,1)} %copy-done.17), channel_id=1, source_target_pairs={{0,8},{4,12},{8,0},{12,4},{1,9},{5,13},{9,1},{13,5},{2,10},{6,14},... | collective-permute-start | bytes 1572872 | tf_op jit(solution)/shard_map/ppermute | solution.py:17
  (71 other events, 1087.2 us)
Sparse Core Ops, SparseCore 0:
  29.0 29.5 reduce-scatter.4
  76.5 24.7 reduce-scatter.6
  160.1 27.9 all-gather.2
  250.6 27.1 reduce-scatter.8
  279.6 26.5 all-gather.4
  353.7 25.8 reduce-scatter.10
